TPU v7x, 128 devices: a whole 4x4x4 slice. The times are simulated.
128 devices in a mesh: seq: 32 (over x_lo, y, z), ch: 4 (over x_hi, core).
Axes of the slice: x: 4 (x_hi: 2, x_lo: 2; x = x_hi * 2 + x_lo), y: 4, z: 4, core: 2. Of those that a mesh axis runs over, the one named last changes fastest.
Arguments:
- projected: bfloat16 [3, 16384, 8192], P(None, 'seq', 'ch'), may hold values from -6 to 6
- short_filters: float32 [3, 3, 8192], P(None, None, 'ch'), may hold values from -3.5 to 3.5
- long_filter: float32 [128, 8192], P(None, 'ch'), may hold values from -0.5 to 0.5
- skip_gain: float32 [8192], P('ch'), may hold values from -4 to 4
- cotangent: bfloat16 [16384, 8192], P(('seq', 'ch')), may hold values from -6 to 6
Outputs:
- grad_input: bfloat16 [3, 16384, 8192], P(None, 'seq', 'ch')
- grad_long: float32 [128, 8192], P(None, 'ch')
- grad_skip: float32 [8192], P('ch')
- grad_short: float32 [3, 3, 8192], P(None, None, 'ch')
All inputs are finite; a program needn't handle non-finite values.
Results may differ from a plain program's by a relative error of at most 0.0057.
Values may be sent and summed in bfloat16 or wider, within the bound.
A program may use at most 128 MiB of HBM per device.

v0:
```python
import jax
import jax.numpy as jnp
from jax import lax
from jax.sharding import PartitionSpec as P

TAPS = 128
SHORT = 3


def passed_along(value, axis, steps):
    count = lax.axis_size(axis)
    initial, last = (max(0, -steps), min(count, count - steps))
    return lax.ppermute(value, axis, [(source, source + steps) for source in range(initial, last)])


def correlate(extended, kernel, accuracy):
    channels = extended.shape[1]
    result = lax.conv_general_dilated(
        extended[None],
        kernel[:, None, :],
        (1,),
        "VALID",
        dimension_numbers=("NWC", "WIO", "NWC"),
        feature_group_count=channels,
        precision=accuracy,
        preferred_element_type=jnp.float32,
    )
    return result[0]


def short_forward(extended, short_filters, count):
    short_lag = SHORT - 1
    streams = jnp.zeros((3, count, extended.shape[2]), jnp.float32)
    for offset in range(SHORT):
        window = extended[:, short_lag - offset : short_lag - offset + count, :].astype(jnp.float32)
        streams = streams + short_filters[:, offset][:, None, :] * window
    return streams


def per_device(projected, short_filters, long_filter, skip_gain, cotangent):
    length = projected.shape[1]
    short_lag = SHORT - 1
    long_reach = TAPS - 1
    highest = lax.Precision.HIGHEST
    before = passed_along(projected[:, length - short_lag :, :], "seq", 1)
    own_input = jnp.concatenate([before, projected], axis=1)
    streams = short_forward(own_input, short_filters, length)
    gated = (streams[1] * streams[2]).astype(jnp.bfloat16)
    gated = lax.optimization_barrier(gated)
    earlier = passed_along(gated[length - long_reach :], "seq", 1)
    gated_ext = jnp.concatenate([earlier, gated], axis=0)
    query_rows, key_rows, value_rows = (streams[0], streams[1], streams[2])
    gated_f = gated_ext.astype(jnp.float32)
    own_gated = gated_f[long_reach:]
    long_mixed = correlate(gated_f, long_filter[::-1], highest) + skip_gain * own_gated
    local_grad = lax.all_to_all(cotangent, "ch", split_axis=1, concat_axis=0, tiled=True)
    upstream = local_grad.astype(jnp.float32)
    d_query = (upstream * long_mixed).astype(jnp.bfloat16)
    d_mixed = (upstream * query_rows).astype(jnp.bfloat16)
    d_mixed = lax.optimization_barrier(d_mixed)
    d_mixed_f = d_mixed.astype(jnp.float32)
    following = passed_along(d_mixed[:long_reach], "seq", -1)
    mixed_ext = jnp.concatenate([d_mixed, following], axis=0).astype(jnp.float32)
    d_gated = correlate(mixed_ext, long_filter, highest) + skip_gain * d_mixed_f
    d_key = (d_gated * value_rows).astype(jnp.bfloat16)
    d_value = (d_gated * key_rows).astype(jnp.bfloat16)
    stream_grads = lax.optimization_barrier(jnp.stack([d_query, d_key, d_value]))
    next_terms = passed_along(stream_grads[:, :short_lag], "seq", -1)
    terms_ext = jnp.concatenate([stream_grads, next_terms], axis=1)
    grad_input = jnp.zeros((3, length, d_mixed.shape[1]), jnp.float32)
    for offset in range(SHORT):
        grad_input = grad_input + short_filters[:, offset][:, None, :] * terms_ext[
            :, offset : offset + length, :
        ].astype(jnp.float32)
    long_partial = correlate(gated_ext, d_mixed, None)[::-1]
    skip_partial = jnp.sum(d_mixed_f * own_gated, axis=0)
    short_partial = jnp.stack(
        [
            jnp.einsum(
                "itc,itc->ic",
                stream_grads,
                own_input[:, short_lag - offset : short_lag - offset + length, :],
                preferred_element_type=jnp.float32,
            )
            for offset in range(SHORT)
        ],
        axis=1,
    )
    reduced = lax.psum((long_partial, skip_partial, short_partial), "seq")
    factor = float(length * lax.axis_size("seq")) ** (-0.5)
    return (
        grad_input.astype(jnp.bfloat16),
        reduced[0] * factor,
        reduced[1] * factor,
        reduced[2] * factor,
    )


def solution(mesh):
    placed = (
        P(None, "seq", "ch"),
        P(None, None, "ch"),
        P(None, "ch"),
        P("ch"),
        P(("seq", "ch"), None),
    )
    return jax.shard_map(
        per_device,
        mesh=mesh,
        in_specs=placed,
        out_specs=(P(None, "seq", "ch"), P(None, "ch"), P("ch"), P(None, None, "ch")),
        check_vma=False,
    )
```

profile of v0, /device:TPU:0, one launch (start us, length us, event | category | flops | bytes accessed | tf_op | source)
XLA Modules:
  0.0 651.9 jit_solution(1923704165718877167)
XLA Ops:
  7.2 1.0 slice.55
  8.1 3.9 collective-permute-start
  12.0 3.2 copy.77
  15.2 4.5 all-to-all-start
  19.7 0.0 all-reduce.3.cloned.1.call-start
  19.7 0.1 fusion.24
  19.9 0.0 collective-permute-done
  19.9 0.0 copy-start.13
  19.9 0.5 copy-done.7
  20.4 0.0 copy-done.9
  20.5 0.0 copy-done.11
  20.5 15.9 %multiply_add_fusion = f32[3,512,2048]{2,1,0:T(8,128)} fusion(bf16[3,512,2048]{2,1,0:T(8,128)(2,1)} %param.5, bf16[3,2,2048]{2,1,0:T(2,128)(2,1)S(1)} %collective-permute-done, f32[3,2048]{1,0:T(4,128)S(1)} %get-tuple-element.22, f32[3,2048]{1,0:T(4,128)S(1)} %get-tuple-element.23, f32[3,2048]{1,0:T(4,128)S(1)} %bitcast.90), kind=kLoop, calls=%fused_computation.7 | loop fusion | flops 44040192 | bytes 18972672 | tf_op jit(solution)/shard_map/add | solution.py:36
  36.4 10.6 %all-to-all-done = bf16[128,4,2048]{2,0,1:T(8,128)(2,1)} async-done(((bf16[128,4,2048]{2,0,1:T(8,128)(2,1)}), bf16[128,4,2048]{2,0,1:T(8,128)(2,1)}, u32[]{:S(2)}, u32[]{:S(2)}) %all-to-all-start) | async-done | bytes 2097184 | tf_op jit(solution)/shard_map/all_to_all | solution.py:56
  46.9 8.3 %multiply_convert_fusion.2 = (bf16[512,2048]{1,0:T(8,128)(2,1)S(1)}, bf16[512,2048]{1,0:T(8,128)(2,1)}) fusion(f32[3,512,2048]{2,1,0:T(8,128)} %multiply_add_fusion, bf16[128,4,2048]{2,0,1:T(8,128)(2,1)} %all-to-all-done), kind=kLoop, calls=%fused_computation.37 | loop fusion | flops 5242880 | bytes 18874368 | tf_op jit(solution)/shard_map/convert_element_type | solution.py:48
  55.3 1.1 slice.72
  56.4 4.6 collective-permute-start.1
  61.0 5.2 rev.6
  66.1 2.0 slice.74
  68.2 1.3 collective-permute-start.2
  69.5 2.0 collective-permute-done.1
  71.5 1.7 maximum_bitcast_fusion
  73.2 0.0 copy-start.6
  73.2 55.0 %fusion.15 = f32[1,128,2048]{2,0,1:T(1,128)} fusion(bf16[512,1,2048]{2,0,1:T(8,128)(2,1)S(1)} %bitcast.84, bf16[1,639,2048]{2,1,0:T(8,128)(2,1)S(1)} %maximum_bitcast_fusion), kind=kOutput, calls=%fused_computation.33 | convolution fusion | flops 268435456 | bytes 5763072 | tf_op jit(solution)/shard_map/conv_general_dilated | solution.py:18
  128.2 45.7 %fusion.18 = f32[1,512,2048]{2,0,1:T(1,128)} fusion(bf16[1,639,2048]{2,1,0:T(8,128)(2,1)S(1)} %maximum_bitcast_fusion, f32[128,1,2048]{2,0,1:T(8,128)S(1)} %bitcast.89), kind=kOutput, calls=%fused_computation.39 | convolution fusion | flops 1610612736 | bytes 7860224 | tf_op jit(solution)/shard_map/conv_general_dilated | solution.py:18
  173.9 0.0 collective-permute-done.2
  173.9 1.5 maximum_bitcast_fusion.1
  175.3 0.0 slice-start.1
  175.3 0.0 slice-start.2
  175.4 0.0 copy-start.16
  175.4 45.6 %fusion.6 = f32[1,512,2048]{2,0,1:T(1,128)} fusion(bf16[1,639,2048]{2,1,0:T(8,128)(2,1)S(1)} %maximum_bitcast_fusion.1, f32[128,1,2048]{2,0,1:T(8,128)S(1)} %bitcast.88), kind=kOutput, calls=%fused_computation.21 | convolution fusion | flops 1610612736 | bytes 7860224 | tf_op jit(solution)/shard_map/conv_general_dilated | solution.py:18
  221.1 7.1 %fusion.20 = (bf16[1,512,2048]{2,1,0:T(8,128)(2,1)S(1)}, bf16[1,512,2048]{2,1,0:T(8,128)(2,1)S(1)}, f32[2048]{0:T(1024)S(1)}, bf16[512,2048]{1,0:T(8,128)(2,1)S(1)}) fusion(f32[3,512,2048]{2,1,0:T(8,128)S(1)} %bitcast.83, bf16[512,2048]{1,0:T(8,128)(2,1)S(1)} %copy-done.2, f32[1,512,2048]{2,0,1:T(1,128)} %fusion.6, f32[2048]{0:T(1024)S(1)} %copy-done.16, ...), kind=kLoop, calls=%fused_computation.43 | loop fusion | flops 15726592 | bytes 29376512 | tf_op jit(solution)/shard_map/stack | solution.py:67
  228.2 0.0 copy-start.14
  228.2 3.1 pad_maximum_fusion.2
  231.4 84.4 %psum.22 = f32[2048]{0:T(1024)S(1)} all-reduce(f32[2048]{0:T(1024)S(1)} %get-tuple-element.17), channel_id=1, replica_groups=mesh['seq'=32,'ch'=4] {'seq'}, use_global_device_ids=true, to_apply=%region_2.0 | all-reduce | flops 2048 | bytes 16384 | tf_op jit(solution)/shard_map/psum | solution.py:89
  315.8 0.9 slice.75
  316.7 1.4 collective-permute-start.3
  318.2 13.8 %fusion.1 = (f32[3,2048]{1,0:T(4,128)S(1)}, f32[3,2048]{1,0:T(4,128)S(1)}, f32[3,2048]{1,0:T(4,128)S(1)}) fusion(bf16[3,512,2048]{2,1,0:T(8,128)(2,1)} %pad_maximum_fusion.2, bf16[3,512,2048]{2,1,0:T(8,128)(2,1)} %param.5, bf16[3,2,2048]{2,1,0:T(2,128)(2,1)S(1)} %copy-done.14), kind=kLoop, calls=%fused_computation.4 | loop fusion | flops 56604672 | bytes 12681216 | tf_op jit(solution)/shard_map/itc,itc->ic/dot_general | solution.py:79
  331.9 0.7 pad_maximum_fusion.3
  332.6 0.6 broadcast_multiply_fusion.2
  333.2 0.3 copy.78
  333.6 5.2 rev.7
  338.7 0.0 all-reduce.3.cloned.1.call-update
  338.8 0.0 collective-permute-done.3
  338.8 14.5 %add_convert_fusion = bf16[3,512,2048]{2,1,0:T(8,128)(2,1)} fusion(bf16[3,512,2048]{2,1,0:T(8,128)(2,1)} %pad_maximum_fusion.2, bf16[3,2,2048]{2,1,0:T(2,128)(2,1)S(1)} %collective-permute-done.3, f32[3,2048]{1,0:T(4,128)S(1)} %copy-done.8, f32[3,2048]{1,0:T(4,128)S(1)} %copy-done.10, f32[3,2048]{1,0:T(4,128)S(1)} %bitcast.91), kind=kLoop, calls=%fused_computation.6 | loop fusion | flops 47185920 | bytes 12681216 | tf_op jit(solution)/shard_map/convert_element_type | solution.py:92
  353.3 287.8 %all-reduce.3.cloned.1.call-done = (f32[128,2048]{1,0:T(8,128)}, f32[3,3,2048]{2,0,1:T(4,128)}) async-done(((f32[128,2048]{1,0:T(8,128)}, f32[3,3,2048]{2,0,1:T(4,128)}), (f32[128,2048]{1,0:T(8,128)}, f32[3,3,2048]{2,0,1:T(4,128)})) %all-reduce.3.cloned.1.call-update) | async-done | bytes 1122320 | tf_op jit(solution)/shard_map/psum | solution.py:89
  641.2 2.3 broadcast_multiply_fusion
  643.5 0.9 broadcast_multiply_fusion.1
  644.4 0.7 copy.21
  (34 shorter events, 0.1 us)
Async XLA Ops:
  7.2 12.6 %copy-start.15 = (f32[3,3,2048]{2,1,0:T(4,128)S(1)}, f32[3,3,2048]{2,1,0:T(4,128)}, u32[]{:S(2)}) copy-start(f32[3,3,2048]{2,1,0:T(4,128)} %param.6) | copy-start | bytes 221188
  8.1 11.8 %collective-permute-start = (bf16[3,2,2048]{2,1,0:T(2,128)(2,1)S(1)}, bf16[3,2,2048]{2,1,0:T(2,128)(2,1)S(1)}, u32[]{:S(2)}, u32[]{:S(2)}) collective-permute-start(bf16[3,2,2048]{2,1,0:T(2,128)(2,1)S(1)} %slice.55), channel_id=1, source_target_pairs={{0,4},{4,8},{8,12},{12,16},{16,20},{20,24},{24,28},{28,32},{32,36}... | collective-permute-start | bytes 73736 | tf_op jit(solution)/shard_map/ppermute | solution.py:13
  15.2 31.7 %all-to-all-start = ((bf16[128,4,2048]{2,0,1:T(8,128)(2,1)}), bf16[128,4,2048]{2,0,1:T(8,128)(2,1)}, u32[]{:S(2)}, u32[]{:S(2)}) async-start(bf16[128,4,2048]{2,0,1:T(8,128)(2,1)} %bitcast.79), calls=%async_computation | async-start | bytes 4194304 | tf_op jit(solution)/shard_map/all_to_all | solution.py:56
  19.7 621.5 %all-reduce.3.cloned.1.call-start = ((), (), s32[]{:S(2)}) async-start(), calls=%async_computation.1 | async-start | bytes 2293760 | tf_op jit(solution)/shard_map/psum | solution.py:89
  19.8 0.6 copy-start.7
  19.8 0.6 copy-start.9
  19.9 0.6 copy-start.11
  19.9 16.5 %copy-start.13 = (bf16[3,2,2048]{2,1,0:T(2,128)(2,1)}, bf16[3,2,2048]{2,1,0:T(2,128)(2,1)S(1)}, u32[]{:S(2)}) copy-start(bf16[3,2,2048]{2,1,0:T(2,128)(2,1)S(1)} %collective-permute-done) | copy-start | bytes 73732
  36.4 24.6 %copy-start.3 = (f32[128,2048]{1,0:T(8,128)S(1)}, f32[128,2048]{1,0:T(8,128)}, u32[]{:S(2)}) copy-start(f32[128,2048]{1,0:T(8,128)} %param.7) | copy-start | bytes 3145732
  55.3 72.9 %copy-start = (bf16[512,2048]{1,0:T(8,128)(2,1)}, bf16[512,2048]{1,0:T(8,128)(2,1)S(1)}, u32[]{:S(2)}) copy-start(bf16[512,2048]{1,0:T(8,128)(2,1)S(1)} %get-tuple-element.15) | copy-start | bytes 6291460
  56.4 15.1 %collective-permute-start.1 = (bf16[127,2048]{1,0:T(8,128)(2,1)}, bf16[127,2048]{1,0:T(8,128)(2,1)}, u32[]{:S(2)}, u32[]{:S(2)}) collective-permute-start(bf16[127,2048]{1,0:T(8,128)(2,1)} %slice.72), channel_id=1, source_target_pairs={{0,4},{4,8},{8,12},{12,16},{16,20},{20,24},{24,28},{28,32},{32,36}... | collective-permute-start | bytes 1560584 | tf_op jit(solution)/shard_map/ppermute | solution.py:13
  66.1 7.0 %copy-start.2 = (bf16[512,2048]{1,0:T(8,128)(2,1)S(1)}, bf16[512,2048]{1,0:T(8,128)(2,1)}, u32[]{:S(2)}) copy-start(bf16[512,2048]{1,0:T(8,128)(2,1)} %get-tuple-element.16) | copy-start | bytes 6291460
  68.2 105.7 %collective-permute-start.2 = (bf16[127,2048]{1,0:T(8,128)(2,1)}, bf16[127,2048]{1,0:T(8,128)(2,1)}, u32[]{:S(2)}, u32[]{:S(2)}) collective-permute-start(bf16[127,2048]{1,0:T(8,128)(2,1)} %slice.74), channel_id=1, source_target_pairs={{4,0},{8,4},{12,8},{16,12},{20,16},{24,20},{28,24},{32,28},{36,32}... | collective-permute-start | bytes 1560584 | tf_op jit(solution)/shard_map/ppermute | solution.py:13
  73.2 55.0 %copy-start.6 = (f32[128,2048]{1,0:T(8,128)S(1)}, f32[128,2048]{1,0:T(8,128)}, u32[]{:S(2)}) copy-start(f32[128,2048]{1,0:T(8,128)} %rev.6) | copy-start | bytes 3145732
  128.2 47.1 %copy-start.4 = (f32[128,2048]{1,0:T(8,128)S(1)}, f32[128,2048]{1,0:T(8,128)}, u32[]{:S(2)}) copy-start(f32[128,2048]{1,0:T(8,128)} %param.7) | copy-start | bytes 3145732
  173.9 47.1 %slice-start = ((s8[12582912]{0:T(1024)(128)(4,1)}), s8[4194304]{0:T(1024)(128)(4,1)S(1)}, s32[]{:S(2)}) async-start(s8[12582912]{0:T(1024)(128)(4,1)} %bitcast.82), calls=%async_computation.2 | async-start | bytes 8388608
  175.3 45.7 %slice-start.1 = ((s8[12582912]{0:T(1024)(128)(4,1)}), s8[4194304]{0:T(1024)(128)(4,1)S(1)}, s32[]{:S(2)}) async-start(s8[12582912]{0:T(1024)(128)(4,1)} %bitcast.82), calls=%async_computation.3 | async-start | bytes 8388608
  175.3 45.7 %slice-start.2 = ((s8[12582912]{0:T(1024)(128)(4,1)}), s8[4194304]{0:T(1024)(128)(4,1)S(1)}, s32[]{:S(2)}) async-start(s8[12582912]{0:T(1024)(128)(4,1)} %bitcast.82), calls=%async_computation.4 | async-start | bytes 8388608
  175.4 45.7 %copy-start.1 = (bf16[512,2048]{1,0:T(8,128)(2,1)S(1)}, bf16[512,2048]{1,0:T(8,128)(2,1)}, u32[]{:S(2)}) copy-start(bf16[512,2048]{1,0:T(8,128)(2,1)} %copy-done) | copy-start | bytes 6291460
  175.4 45.7 %copy-start.16 = (f32[2048]{0:T(1024)S(1)}, f32[2048]{0:T(1024)}, u32[]{:S(2)}) copy-start(f32[2048]{0:T(1024)} %param.8) | copy-start | bytes 24580
  228.2 89.9 %copy-start.14 = (bf16[3,2,2048]{2,1,0:T(2,128)(2,1)S(1)}, bf16[3,2,2048]{2,1,0:T(2,128)(2,1)}, u32[]{:S(2)}) copy-start(bf16[3,2,2048]{2,1,0:T(2,128)(2,1)} %copy-done.13) | copy-start | bytes 73732
  316.7 16.5 %copy-start.5 = (f32[1,128,2048]{2,0,1:T(1,128)S(1)}, f32[1,128,2048]{2,0,1:T(1,128)}, u32[]{:S(2)}) copy-start(f32[1,128,2048]{2,0,1:T(1,128)} %fusion.15) | copy-start | bytes 3145732
  316.7 22.1 %copy-start.8 = (f32[3,2048]{1,0:T(4,128)S(1)}, f32[3,2048]{1,0:T(4,128)}, u32[]{:S(2)}) copy-start(f32[3,2048]{1,0:T(4,128)} %copy-done.7) | copy-start | bytes 73732
  316.7 22.1 %copy-start.10 = (f32[3,2048]{1,0:T(4,128)S(1)}, f32[3,2048]{1,0:T(4,128)}, u32[]{:S(2)}) copy-start(f32[3,2048]{1,0:T(4,128)} %copy-done.9) | copy-start | bytes 73732
  316.7 22.1 %copy-start.12 = (f32[3,1,2048]{2,0,1:T(4,128)S(1)}, f32[3,1,2048]{2,0,1:T(4,128)}, u32[]{:S(2)}) copy-start(f32[3,1,2048]{2,0,1:T(4,128)} %copy-done.11) | copy-start | bytes 73732
  316.7 22.0 %collective-permute-start.3 = (bf16[3,2,2048]{2,1,0:T(2,128)(2,1)S(1)}, bf16[3,2,2048]{2,1,0:T(2,128)(2,1)S(1)}, u32[]{:S(2)}, u32[]{:S(2)}) collective-permute-start(bf16[3,2,2048]{2,1,0:T(2,128)(2,1)S(1)} %slice.75), channel_id=1, source_target_pairs={{4,0},{8,4},{12,8},{16,12},{20,16},{24,20},{28,24},{32,28},{36,32}... | collective-permute-start | bytes 73736 | tf_op jit(solution)/shard_map/ppermute | solution.py:13
Sparse Core Ops, SparseCore 0:
  338.9 302.2 all-reduce.2
where the time goes:
time: 652 us
  waiting for transfers between devices  300 us (46%)
  matrix products  146 us (22%)
  blocking collectives  84.4 us (13%)
  other arithmetic  70.4 us (11%)
  local copies, waits for them, and re-layouts  20.3 us (3%)
  starting transfers between devices  15.7 us (2%)
  between operations  14.4 us (2%)
    psum x1, waiting for transfers between devices, per_device(): reduced = lax.psum((long_partial, skip_partial, short_partial), 'seq')  288 us
    conv_general_dilated x3, matrix products, correlate(): lax.conv_general_dilated(extended[None], kernel[:, None, :], (1,), 'VALID...  146 us
    psum x1, blocking collectives, per_device(): reduced = lax.psum((long_partial, skip_partial, short_partial), 'seq')  84.4 us
    add x1, other arithmetic, short_forward(): streams = streams + short_filters[:, offset][:, None, :] * window  15.9 us
    convert_element_type x1, other arithmetic, per_device(): grad_input.astype(jnp.bfloat16)  14.5 us
    dot_general x1, other arithmetic, per_device(): jnp.einsum('itc,itc->ic', stream_grads, own_input[:, short_lag - offset:s...  13.8 us
  transfers between devices with their start and end apart: 6, of which 3 were waited for; matrix products, arithmetic and copies ran while one was open for 25% of the time, Pallas kernels for 0%

commit v1 on v0

--- a/solution.py
+++ b/solution.py
@@ -1,6 +1,8 @@
 import jax
 import jax.numpy as jnp
 from jax import lax
+from jax.experimental import pallas as pl
+from jax.experimental.pallas import tpu as pltpu
 from jax.sharding import PartitionSpec as P
 
 TAPS = 128
@@ -35,6 +37,87 @@
         window = extended[:, short_lag - offset : short_lag - offset + count, :].astype(jnp.float32)
         streams = streams + short_filters[:, offset][:, None, :] * window
     return streams
+
+
+PEERS = 32
+PIECE = 1152
+MESH = pl.DeviceIdType.MESH
+
+
+def all_reduce_kernel(long_ref, rest_ref, long_out, rest_out, parts, landed, total, gathered, sems):
+    me = lax.axis_index("seq")
+    barrier = pltpu.get_barrier_semaphore()
+
+    @pl.loop(1, PEERS)
+    def _(k):
+        pl.semaphore_signal(barrier, inc=1, device_id={"seq": lax.rem(me + k, PEERS)}, device_id_type=MESH)
+
+    for p in range(PEERS):
+        row, half = p // 2, p % 2
+        parts[p, :, :1024] = long_ref[8 * row : 8 * row + 8, 1024 * half : 1024 * half + 1024]
+        row, tile = p // 16, p % 16
+        parts[p, :, 1024:] = rest_ref[8 * row : 8 * row + 8, 128 * tile : 128 * tile + 128]
+    pl.semaphore_wait(barrier, PEERS - 1)
+
+    @pl.loop(1, PEERS)
+    def _(k):
+        peer = lax.rem(me + k, PEERS)
+        pltpu.make_async_remote_copy(
+            src_ref=parts.at[peer],
+            dst_ref=landed.at[k - 1],
+            send_sem=sems.at[0],
+            recv_sem=sems.at[1],
+            device_id={"seq": peer},
+            device_id_type=MESH,
+        ).start()
+
+    pltpu.make_async_copy(landed, landed, sems.at[1]).wait()
+    acc = parts[me]
+    for k in range(PEERS - 1):
+        acc = acc + landed[k]
+    total[...] = acc
+    gathered[me] = acc
+
+    @pl.loop(1, PEERS)
+    def _(k):
+        peer = lax.rem(me + k, PEERS)
+        pltpu.make_async_remote_copy(
+            src_ref=total,
+            dst_ref=gathered.at[me],
+            send_sem=sems.at[2],
+            recv_sem=sems.at[3],
+            device_id={"seq": peer},
+            device_id_type=MESH,
+        ).start()
+
+    pltpu.make_async_copy(landed, landed, sems.at[0]).wait()
+    pltpu.make_async_copy(landed, landed, sems.at[3]).wait()
+    pltpu.make_async_copy(landed, landed, sems.at[2]).wait()
+    for p in range(PEERS):
+        row, half = p // 2, p % 2
+        long_out[8 * row : 8 * row + 8, 1024 * half : 1024 * half + 1024] = gathered[p, :, :1024]
+        row, tile = p // 16, p % 16
+        rest_out[8 * row : 8 * row + 8, 128 * tile : 128 * tile + 128] = gathered[p, :, 1024:]
+
+
+def all_reduce(long_partial, rest):
+    return pl.pallas_call(
+        all_reduce_kernel,
+        out_shape=(
+            jax.ShapeDtypeStruct(long_partial.shape, jnp.float32),
+            jax.ShapeDtypeStruct(rest.shape, jnp.float32),
+        ),
+        in_specs=[pl.BlockSpec(memory_space=pltpu.VMEM)] * 2,
+        out_specs=[pl.BlockSpec(memory_space=pltpu.VMEM)] * 2,
+        scratch_shapes=[
+            pltpu.VMEM((PEERS, 8, PIECE), jnp.float32),
+            pltpu.VMEM((PEERS - 1, 8, PIECE), jnp.float32),
+            pltpu.VMEM((8, PIECE), jnp.float32),
+            pltpu.VMEM((PEERS, 8, PIECE), jnp.float32),
+            pltpu.SemaphoreType.DMA((4,)),
+        ],
+        compiler_params=pltpu.CompilerParams(collective_id=0, has_side_effects=True, vmem_limit_bytes=32 << 20),
+    )(long_partial, rest)
 
 
 def per_device(projected, short_filters, long_filter, skip_gain, cotangent):
@@ -86,7 +169,9 @@
         ],
         axis=1,
     )
-    reduced = lax.psum((long_partial, skip_partial, short_partial), "seq")
+    rest = jnp.concatenate([skip_partial[None], short_partial.reshape(9, -1), jnp.zeros((6, skip_partial.shape[0]), jnp.float32)])
+    long_sum, rest_sum = all_reduce(long_partial.reshape(TAPS, -1), rest)
+    reduced = (long_sum, rest_sum[0], rest_sum[1:10].reshape(3, SHORT, -1))
     factor = float(length * lax.axis_size("seq")) ** (-0.5)
     return (
         grad_input.astype(jnp.bfloat16),

time: 652 us -> 301 us (0.46)
  waiting for transfers between devices: 300 us -> 11.9 us
  blocking collectives: 84.4 us -> 0 us
  Pallas kernels: 0 us -> 39.2 us
  between operations: 14.4 us -> 1.11 us
  other arithmetic: 70.4 us -> 61.6 us
    psum x1 -> x0, waiting for transfers between devices: 288 us -> none  [per_device(): reduced = lax.psum((long_partial, skip_partial, short_partial), 'seq')]
    psum x1 -> x0, blocking collectives: 84.4 us -> none  [per_device(): reduced = lax.psum((long_partial, skip_partial, short_partial), 'seq')]
    pallas_call x0 -> x1, Pallas kernels: none -> 39.2 us  [all_reduce(): pl.pallas_call(all_reduce_kernel, out_shape=(jax.ShapeDtypeStruct(long_pa...]
    dot_general x1, other arithmetic: 13.8 us -> 5.52 us  [per_device(): jnp.einsum('itc,itc->ic', stream_grads, own_input[:, short_lag - offset:s...]
  transfers between devices with their start and end apart: 6 -> 5, of which waited for: 3 -> 2; matrix products, arithmetic and copies ran while one was open for 25% -> 48% of each run, Pallas kernels for 0% -> 13%
where the time goes in v1:
time: 301 us; the launch traced here: 299 us
  matrix products  147 us (49%)
  other arithmetic  61.6 us (20%)
  Pallas kernels  39.2 us (13%)
  local copies, waits for them, and re-layouts  22.7 us (8%)
  starting transfers between devices  15.9 us (5%)
  waiting for transfers between devices  11.9 us (4%)
    conv_general_dilated x3, matrix products, correlate(): lax.conv_general_dilated(extended[None], kernel[:, None, :], (1,), 'VALID...  147 us
    pallas_call x1, Pallas kernels, all_reduce(): pl.pallas_call(all_reduce_kernel, out_shape=(jax.ShapeDtypeStruct(long_pa...  39.2 us
    add x1, other arithmetic, short_forward(): streams = streams + short_filters[:, offset][:, None, :] * window  15.9 us
    convert_element_type x1, other arithmetic, per_device(): grad_input.astype(jnp.bfloat16)  14.4 us
    another operation x2, other arithmetic, per_device(): jnp.stack([d_query, d_key, d_value])  12.5 us
    ppermute x4, starting transfers between devices, passed_along(): lax.ppermute(value, axis, [(source, source + steps) for source in range(i...  11.4 us
    all_to_all x1, waiting for transfers between devices, per_device(): lax.all_to_all(cotangent, 'ch', split_axis=1, concat_axis=0, tiled=True)  10.6 us
    convert_element_type x1, other arithmetic, per_device(): gated = (streams[1] * streams[2]).astype(jnp.bfloat16)  8.33 us
  transfers between devices with their start and end apart: 5, of which 2 were waited for; matrix products, arithmetic and copies ran while one was open for 48% of the time, Pallas kernels for 13%

profile of v1, /device:TPU:0, one launch (start us, length us, event | category | flops | bytes accessed | tf_op | source)
XLA Modules:
  0.0 299.1 jit_solution(9909668163779900334)
XLA Ops:
  0.6 1.0 slice.61
  1.6 3.9 %collective-permute-start = (bf16[3,2,2048]{2,1,0:T(2,128)(2,1)S(1)}, bf16[3,2,2048]{2,1,0:T(2,128)(2,1)S(1)}, u32[]{:S(2)}, u32[]{:S(2)}) collective-permute-start(bf16[3,2,2048]{2,1,0:T(2,128)(2,1)S(1)} %slice.61), channel_id=1, source_target_pairs={{0,4},{4,8},{8,12},{12,16},{16,20},{20,24},{24,28},{28,32},{32,36}... | collective-permute-start | bytes 73736 | tf_op jit(solution)/shard_map/ppermute | solution.py:15
  5.5 3.2 %copy.76 = bf16[16,4,8,2048]{3,2,0,1:T(8,128)(2,1)} copy(bf16[16,4,8,2048]{3,2,1,0:T(8,128)(2,1)} %bitcast.88) | data formatting | bytes 4194304 | tf_op jit(solution)/shard_map/all_to_all | solution.py:139
  8.7 4.5 %all-to-all-start = ((bf16[128,4,2048]{2,0,1:T(8,128)(2,1)}), bf16[128,4,2048]{2,0,1:T(8,128)(2,1)}, u32[]{:S(2)}, u32[]{:S(2)}) async-start(bf16[128,4,2048]{2,0,1:T(8,128)(2,1)} %bitcast.78), calls=%async_computation | async-start | bytes 4194304 | tf_op jit(solution)/shard_map/all_to_all | solution.py:139
  13.2 0.1 fusion.24
  13.3 0.0 collective-permute-done
  13.3 0.0 copy-start.13
  13.3 0.5 copy-done.7
  13.9 0.0 copy-done.11
  13.9 15.9 %multiply_add_fusion = f32[3,512,2048]{2,1,0:T(8,128)} fusion(bf16[3,512,2048]{2,1,0:T(8,128)(2,1)} %param.5, bf16[3,2,2048]{2,1,0:T(2,128)(2,1)S(1)} %collective-permute-done, f32[3,2048]{1,0:T(4,128)S(1)} %get-tuple-element.20, f32[3,2048]{1,0:T(4,128)S(1)} %get-tuple-element.21, f32[3,2048]{1,0:T(4,128)S(1)} %bitcast.91), kind=kLoop, calls=%fused_computation.7 | loop fusion | flops 44040192 | bytes 18972672 | tf_op jit(solution)/shard_map/add | solution.py:38
  29.8 10.6 %all-to-all-done = bf16[128,4,2048]{2,0,1:T(8,128)(2,1)} async-done(((bf16[128,4,2048]{2,0,1:T(8,128)(2,1)}), bf16[128,4,2048]{2,0,1:T(8,128)(2,1)}, u32[]{:S(2)}, u32[]{:S(2)}) %all-to-all-start) | async-done | bytes 2097184 | tf_op jit(solution)/shard_map/all_to_all | solution.py:139
  40.4 8.3 %multiply_convert_fusion.2 = (bf16[512,2048]{1,0:T(8,128)(2,1)S(1)}, bf16[512,2048]{1,0:T(8,128)(2,1)}) fusion(f32[3,512,2048]{2,1,0:T(8,128)} %multiply_add_fusion, bf16[128,4,2048]{2,0,1:T(8,128)(2,1)} %all-to-all-done), kind=kLoop, calls=%fused_computation.37 | loop fusion | flops 5242880 | bytes 18874368 | tf_op jit(solution)/shard_map/convert_element_type | solution.py:131
  48.7 1.1 slice.80
  49.9 4.6 %collective-permute-start.1 = (bf16[127,2048]{1,0:T(8,128)(2,1)}, bf16[127,2048]{1,0:T(8,128)(2,1)}, u32[]{:S(2)}, u32[]{:S(2)}) collective-permute-start(bf16[127,2048]{1,0:T(8,128)(2,1)} %slice.80), channel_id=1, source_target_pairs={{0,4},{4,8},{8,12},{12,16},{16,20},{20,24},{24,28},{28,32},{32,36}... | collective-permute-start | bytes 1560584 | tf_op jit(solution)/shard_map/ppermute | solution.py:15
  54.5 5.2 %rev.6 = f32[128,2048]{1,0:T(8,128)} reverse(f32[128,2048]{1,0:T(8,128)S(1)} %copy-done.5), dimensions={0} | reverse | bytes 2097152 | tf_op jit(solution)/shard_map/rev | solution.py:138
  59.7 0.6 pad.2.clone
  60.2 1.9 slice.82
  62.2 1.5 collective-permute-start.2
  63.7 1.3 collective-permute-done.1
  65.0 1.7 maximum_bitcast_fusion
  66.7 0.0 copy-start.6
  66.7 54.2 %fusion.15 = f32[1,128,2048]{2,0,1:T(1,128)S(1)} fusion(bf16[512,1,2048]{2,0,1:T(8,128)(2,1)S(1)} %bitcast.85, bf16[1,639,2048]{2,1,0:T(8,128)(2,1)S(1)} %maximum_bitcast_fusion), kind=kOutput, calls=%fused_computation.33 | convolution fusion | flops 268435456 | bytes 5763072 | tf_op jit(solution)/shard_map/conv_general_dilated | solution.py:20
  120.9 0.0 copy-start.4
  121.0 45.7 %fusion.18 = f32[1,512,2048]{2,0,1:T(1,128)} fusion(bf16[1,639,2048]{2,1,0:T(8,128)(2,1)S(1)} %maximum_bitcast_fusion, f32[128,1,2048]{2,0,1:T(8,128)S(1)} %bitcast.90), kind=kOutput, calls=%fused_computation.39 | convolution fusion | flops 1610612736 | bytes 7860224 | tf_op jit(solution)/shard_map/conv_general_dilated | solution.py:20
  166.6 1.3 copy.77
  167.9 6.8 %rev.7.long_ref = f32[128,2048]{1,0:T(8,128)S(1)} reverse(f32[128,2048]{1,0:T(8,128)} %bitcast.87), dimensions={0} | reverse | bytes 2097152 | tf_op jit(solution)/shard_map/rev | solution.py:158
  174.8 0.0 collective-permute-done.2
  174.8 0.0 slice-start
  174.8 0.0 slice-start.3
  174.8 1.5 maximum_bitcast_fusion.1
  176.3 0.0 slice-start.1
  176.3 0.0 slice-start.2
  176.3 0.0 copy-start.16
  176.3 0.0 slice-start.4
  176.3 46.9 %fusion.6 = f32[1,512,2048]{2,0,1:T(1,128)} fusion(bf16[1,639,2048]{2,1,0:T(8,128)(2,1)S(1)} %maximum_bitcast_fusion.1, f32[128,1,2048]{2,0,1:T(8,128)} %bitcast.89), kind=kOutput, calls=%fused_computation.21 | convolution fusion | flops 1610612736 | bytes 7860224 | tf_op jit(solution)/shard_map/conv_general_dilated | solution.py:20
  223.3 8.8 %fusion.20 = (bf16[1,512,2048]{2,1,0:T(8,128)(2,1)}, bf16[1,512,2048]{2,1,0:T(8,128)(2,1)}, f32[2048]{0:T(1024)S(1)}, bf16[512,2048]{1,0:T(8,128)(2,1)}) fusion(f32[3,512,2048]{2,1,0:T(8,128)S(1)} %bitcast.82, bf16[512,2048]{1,0:T(8,128)(2,1)S(1)} %copy-done.4, f32[1,512,2048]{2,0,1:T(1,128)} %fusion.6, f32[2048]{0:T(1024)S(1)} %copy-done.16, ...), kind=kLoop, calls=%fused_computation.43 | loop fusion | flops 15726592 | bytes 29376512 | tf_op jit(solution)/shard_map/stack | solution.py:150
  232.1 3.7 %pad_maximum_fusion.2 = bf16[3,512,2048]{2,1,0:T(8,128)(2,1)S(1)} fusion(bf16[1,512,2048]{2,1,0:T(8,128)(2,1)} %get-tuple-element.12, bf16[1,512,2048]{2,1,0:T(8,128)(2,1)} %get-tuple-element.11, bf16[1,512,2048]{2,1,0:T(8,128)(2,1)} %bitcast.86), kind=kLoop, calls=%fused_computation.17 | loop fusion | flops 6291456 | bytes 12582912 | tf_op jit(solution)/shard_map/stack | solution.py:150
  235.8 0.0 copy-start.17
  235.9 1.4 collective-permute-start.3
  237.3 5.5 %fusion.1 = (f32[3,2048]{1,0:T(4,128)S(1)}, f32[3,2048]{1,0:T(4,128)S(1)}, f32[3,2048]{1,0:T(4,128)S(1)}) fusion(bf16[3,512,2048]{2,1,0:T(8,128)(2,1)S(1)} %pad_maximum_fusion.2, bf16[3,512,2048]{2,1,0:T(8,128)(2,1)S(1)} %bitcast.84, bf16[3,2,2048]{2,1,0:T(2,128)(2,1)S(1)} %copy-done.14), kind=kLoop, calls=%fused_computation.4 | loop fusion | flops 56604672 | bytes 12681216 | tf_op jit(solution)/shard_map/itc,itc->ic/dot_general | solution.py:162
  242.9 0.1 pad_maximum_fusion.3
  243.1 0.1 maximum_maximum_fusion.rest_ref
  243.2 39.2 %shard_map.84 = (f32[128,2048]{1,0:T(8,128)S(1)}, f32[16,2048]{1,0:T(8,128)S(1)}) custom-call(f32[128,2048]{1,0:T(8,128)S(1)} %rev.7.long_ref, f32[16,2048]{1,0:T(8,128)S(1)} %maximum_maximum_fusion.rest_ref), custom_call_target="tpu_custom_call" | custom-call | tf_op jit(solution)/shard_map/pallas_call | solution.py:104
  282.3 1.1 broadcast_multiply_fusion
  283.4 0.6 slice_multiply_fusion.1
  284.0 0.7 mul.132
  284.7 0.0 collective-permute-done.3
  284.7 14.4 %add_convert_fusion = bf16[3,512,2048]{2,1,0:T(8,128)(2,1)} fusion(bf16[3,512,2048]{2,1,0:T(8,128)(2,1)} %copy-done, bf16[3,2,2048]{2,1,0:T(2,128)(2,1)S(1)} %collective-permute-done.3, f32[3,2048]{1,0:T(4,128)S(1)} %copy-done.8, f32[3,2048]{1,0:T(4,128)S(1)} %copy-done.10, f32[3,2048]{1,0:T(4,128)S(1)} %bitcast.92), kind=kLoop, calls=%fused_computation.6 | loop fusion | flops 47185920 | bytes 12681216 | tf_op jit(solution)/shard_map/convert_element_type | solution.py:177
  (45 shorter events, 0.2 us)
Async XLA Ops:
  0.6 12.5 %copy-start.15 = (f32[3,3,2048]{2,1,0:T(4,128)S(1)}, f32[3,3,2048]{2,1,0:T(4,128)}, u32[]{:S(2)}) copy-start(f32[3,3,2048]{2,1,0:T(4,128)} %param.6) | copy-start | bytes 221188
  1.6 11.7 %collective-permute-start = (bf16[3,2,2048]{2,1,0:T(2,128)(2,1)S(1)}, bf16[3,2,2048]{2,1,0:T(2,128)(2,1)S(1)}, u32[]{:S(2)}, u32[]{:S(2)}) collective-permute-start(bf16[3,2,2048]{2,1,0:T(2,128)(2,1)S(1)} %slice.61), channel_id=1, source_target_pairs={{0,4},{4,8},{8,12},{12,16},{16,20},{20,24},{24,28},{28,32},{32,36}... | collective-permute-start | bytes 73736 | tf_op jit(solution)/shard_map/ppermute | solution.py:15
  8.7 31.7 %all-to-all-start = ((bf16[128,4,2048]{2,0,1:T(8,128)(2,1)}), bf16[128,4,2048]{2,0,1:T(8,128)(2,1)}, u32[]{:S(2)}, u32[]{:S(2)}) async-start(bf16[128,4,2048]{2,0,1:T(8,128)(2,1)} %bitcast.78), calls=%async_computation | async-start | bytes 4194304 | tf_op jit(solution)/shard_map/all_to_all | solution.py:139
  13.2 0.6 copy-start.7
  13.3 0.6 copy-start.9
  13.3 0.6 copy-start.11
  13.3 16.5 %copy-start.13 = (bf16[3,2,2048]{2,1,0:T(2,128)(2,1)}, bf16[3,2,2048]{2,1,0:T(2,128)(2,1)S(1)}, u32[]{:S(2)}) copy-start(bf16[3,2,2048]{2,1,0:T(2,128)(2,1)S(1)} %collective-permute-done) | copy-start | bytes 73732
  29.8 24.7 %copy-start.5 = (f32[128,2048]{1,0:T(8,128)S(1)}, f32[128,2048]{1,0:T(8,128)}, u32[]{:S(2)}) copy-start(f32[128,2048]{1,0:T(8,128)} %param.7) | copy-start | bytes 3145732
  48.7 72.2 %copy-start.1 = (bf16[512,2048]{1,0:T(8,128)(2,1)}, bf16[512,2048]{1,0:T(8,128)(2,1)S(1)}, u32[]{:S(2)}) copy-start(bf16[512,2048]{1,0:T(8,128)(2,1)S(1)} %get-tuple-element.13) | copy-start | bytes 6291460
  49.9 15.1 %collective-permute-start.1 = (bf16[127,2048]{1,0:T(8,128)(2,1)}, bf16[127,2048]{1,0:T(8,128)(2,1)}, u32[]{:S(2)}, u32[]{:S(2)}) collective-permute-start(bf16[127,2048]{1,0:T(8,128)(2,1)} %slice.80), channel_id=1, source_target_pairs={{0,4},{4,8},{8,12},{12,16},{16,20},{20,24},{24,28},{28,32},{32,36}... | collective-permute-start | bytes 1560584 | tf_op jit(solution)/shard_map/ppermute | solution.py:15
  59.7 7.0 %copy-start.3 = (bf16[512,2048]{1,0:T(8,128)(2,1)S(1)}, bf16[512,2048]{1,0:T(8,128)(2,1)}, u32[]{:S(2)}) copy-start(bf16[512,2048]{1,0:T(8,128)(2,1)} %get-tuple-element.14) | copy-start | bytes 6291460
  62.2 112.6 %collective-permute-start.2 = (bf16[127,2048]{1,0:T(8,128)(2,1)}, bf16[127,2048]{1,0:T(8,128)(2,1)}, u32[]{:S(2)}, u32[]{:S(2)}) collective-permute-start(bf16[127,2048]{1,0:T(8,128)(2,1)} %slice.82), channel_id=1, source_target_pairs={{4,0},{8,4},{12,8},{16,12},{20,16},{24,20},{28,24},{32,28},{36,32}... | collective-permute-start | bytes 1560584 | tf_op jit(solution)/shard_map/ppermute | solution.py:15
  66.7 54.3 %copy-start.6 = (f32[128,2048]{1,0:T(8,128)S(1)}, f32[128,2048]{1,0:T(8,128)}, u32[]{:S(2)}) copy-start(f32[128,2048]{1,0:T(8,128)} %rev.6) | copy-start | bytes 3145732
  120.9 53.8 %copy-start.4 = (bf16[512,2048]{1,0:T(8,128)(2,1)S(1)}, bf16[512,2048]{1,0:T(8,128)(2,1)}, u32[]{:S(2)}) copy-start(bf16[512,2048]{1,0:T(8,128)(2,1)} %get-tuple-element.14) | copy-start | bytes 6291460
  174.8 48.5 %slice-start = ((s8[12582912]{0:T(1024)(128)(4,1)}), s8[4194304]{0:T(1024)(128)(4,1)S(1)}, s32[]{:S(2)}) async-start(s8[12582912]{0:T(1024)(128)(4,1)} %bitcast.81), calls=%async_computation.1 | async-start | bytes 8388608
  174.8 62.5 %slice-start.3 = ((s8[6291456]{0:T(1024)(128)(4,1)}), s8[4194304]{0:T(1024)(128)(4,1)S(1)}, s32[]{:S(2)}) async-start(s8[6291456]{0:T(1024)(128)(4,1)} %bitcast.83), calls=%async_computation.4 | async-start | bytes 8388608
  176.3 47.0 %slice-start.1 = ((s8[12582912]{0:T(1024)(128)(4,1)}), s8[4194304]{0:T(1024)(128)(4,1)S(1)}, s32[]{:S(2)}) async-start(s8[12582912]{0:T(1024)(128)(4,1)} %bitcast.81), calls=%async_computation.2 | async-start | bytes 8388608
  176.3 47.0 %slice-start.2 = ((s8[12582912]{0:T(1024)(128)(4,1)}), s8[4194304]{0:T(1024)(128)(4,1)S(1)}, s32[]{:S(2)}) async-start(s8[12582912]{0:T(1024)(128)(4,1)} %bitcast.81), calls=%async_computation.3 | async-start | bytes 8388608
  176.3 47.0 %copy-start.2 = (bf16[512,2048]{1,0:T(8,128)(2,1)S(1)}, bf16[512,2048]{1,0:T(8,128)(2,1)}, u32[]{:S(2)}) copy-start(bf16[512,2048]{1,0:T(8,128)(2,1)} %copy-done.1) | copy-start | bytes 6291460
  176.3 47.0 %copy-start.16 = (f32[2048]{0:T(1024)S(1)}, f32[2048]{0:T(1024)}, u32[]{:S(2)}) copy-start(f32[2048]{0:T(1024)} %param.8) | copy-start | bytes 24580
  176.3 61.0 %slice-start.4 = ((s8[6291456]{0:T(1024)(128)(4,1)}), s8[2097152]{0:T(1024)(128)(4,1)S(1)}, s32[]{:S(2)}) async-start(s8[6291456]{0:T(1024)(128)(4,1)} %bitcast.83), calls=%async_computation.5 | async-start | bytes 4194304
  232.1 5.2 %copy-start.14 = (bf16[3,2,2048]{2,1,0:T(2,128)(2,1)S(1)}, bf16[3,2,2048]{2,1,0:T(2,128)(2,1)}, u32[]{:S(2)}) copy-start(bf16[3,2,2048]{2,1,0:T(2,128)(2,1)} %copy-done.13) | copy-start | bytes 73732
  235.8 7.1 %copy-start = (bf16[3,512,2048]{2,1,0:T(8,128)(2,1)}, bf16[3,512,2048]{2,1,0:T(8,128)(2,1)S(1)}, u32[]{:S(2)}) copy-start(bf16[3,512,2048]{2,1,0:T(8,128)(2,1)S(1)} %pad_maximum_fusion.2) | copy-start | bytes 18874372
  235.8 7.3 %copy-start.17 = (f32[16]{0:T(128)S(1)}, f32[16]{0:T(128)}, u32[]{:S(2)}) copy-start(f32[16]{0:T(128)} %pad.2.clone) | copy-start | bytes 196
  235.8 48.9 %copy-start.8 = (f32[3,2048]{1,0:T(4,128)S(1)}, f32[3,2048]{1,0:T(4,128)}, u32[]{:S(2)}) copy-start(f32[3,2048]{1,0:T(4,128)} %copy-done.7) | copy-start | bytes 73732
  235.8 48.9 %copy-start.10 = (f32[3,2048]{1,0:T(4,128)S(1)}, f32[3,2048]{1,0:T(4,128)}, u32[]{:S(2)}) copy-start(f32[3,2048]{1,0:T(4,128)} %copy-done.9) | copy-start | bytes 73732
  235.9 48.9 %copy-start.12 = (f32[3,1,2048]{2,0,1:T(4,128)S(1)}, f32[3,1,2048]{2,0,1:T(4,128)}, u32[]{:S(2)}) copy-start(f32[3,1,2048]{2,0,1:T(4,128)} %copy-done.11) | copy-start | bytes 73732
  235.9 48.8 %collective-permute-start.3 = (bf16[3,2,2048]{2,1,0:T(2,128)(2,1)S(1)}, bf16[3,2,2048]{2,1,0:T(2,128)(2,1)S(1)}, u32[]{:S(2)}, u32[]{:S(2)}) collective-permute-start(bf16[3,2,2048]{2,1,0:T(2,128)(2,1)S(1)} %slice.83), channel_id=1, source_target_pairs={{4,0},{8,4},{12,8},{16,12},{20,16},{24,20},{28,24},{32,28},{36,32}... | collective-permute-start | bytes 73736 | tf_op jit(solution)/shard_map/ppermute | solution.py:15

commit v2 on v0

v2 whole, which is shorter than its diff:
```python
import functools

import jax
import jax.numpy as jnp
import numpy as np
from jax import lax
from jax.experimental import pallas as pl
from jax.experimental.pallas import tpu as pltpu
from jax.sharding import PartitionSpec as P

TAPS = 128
SHORT = 3
TOK = 512
CH = 2048
POINTS = TOK + TAPS
HALF = POINTS // 2
GROUP = 16
PEERS = 32
PARTS = 4
L = CH // PARTS
LT = L // 128
MESH = pl.DeviceIdType.MESH
F32, BF16 = jnp.float32, jnp.bfloat16


def split(x):
    high = x.astype(np.float32).astype(BF16)
    return high, (x - high.astype(np.float64)).astype(np.float32).astype(BF16)


@functools.cache
def matrices():
    angle = 2 * np.pi * np.outer(np.arange(HALF) + 0.5, np.arange(POINTS)) / POINTS
    forward = np.concatenate([np.cos(angle), -np.sin(angle)])
    inverse = (2.0 / POINTS) * np.concatenate([np.cos(angle.T), -np.sin(angle.T)], axis=1)
    fh, fl = split(forward)
    cat = lambda *parts: np.concatenate(parts, axis=1)
    first, last = slice(0, TAPS), slice(TOK, POINTS)

    def back(rows):
        high, low = split(inverse[rows])
        return cat(high, high, low)

    return (
        fh,
        fl,
        cat(fh[:, first], fl[:, first]),
        cat(fh[:, last], fl[:, last]),
        cat(fh[:, first], fl[:, first], fh[:, first]),
        back(np.arange(TAPS, POINTS)),
        back(np.arange(TOK)),
        back(TAPS - np.arange(TAPS)),
    )


def dot(a, b):
    return jnp.dot(a, b, preferred_element_type=F32)


def kernel(
    proj, sf_ref, h_hbm, skip_ref, cot_hbm, m0, m1, m2, m3, m4, m5, m6, m7,
    gi_out, gl_out, gs_out,
    px, qs, ks, vs, gated, g_halo, ghat, hhat, mixed, cot, dm, dm_halo, dhat, ds, d_halo,
    yb, hb, twice, hv, f0, f1, f2, f3, f4, f5, f6, f7,
    parts, landed, xs, xr, sums, gs, gs_landed, gs_x, gs_xr, gs_sums,
    load_sem, mat_sem, h_sem, own_sem, out_sem, a2a_send, a2a_recv,
    ph_sem, gh_sem, dmh_sem, dh_sem, rs_sem, xx_sem, ag_sem, tail_sem,
):
    me = lax.axis_index("seq")
    col = lax.axis_index("ch")
    g = lax.rem(me, GROUP)
    plane = me - g
    nxt, prv = lax.rem(me + 1, PEERS), lax.rem(me + PEERS - 1, PEERS)
    across = lax.rem(me + GROUP, PEERS)
    barrier = pltpu.get_barrier_semaphore()

    def to_seq(s):
        return dict(device_id={"seq": s}, device_id_type=MESH)

    def to_ch(c):
        return dict(device_id={"ch": c}, device_id_type=MESH)

    def mate(k):
        return plane + lax.rem(g + k, GROUP)

    @pl.loop(1, GROUP)
    def _(k):
        pl.semaphore_signal(barrier, inc=1, **to_seq(mate(k)))

    for s in (nxt, prv, across):
        pl.semaphore_signal(barrier, inc=1, **to_seq(s))
    for k in range(1, 4):
        pl.semaphore_signal(barrier, inc=1, **to_ch(lax.rem(col + k, 4)))

    def lanes(c):
        return pl.ds(pl.multiple_of(c * L, L), L)

    def p_load(c):
        return pltpu.make_async_copy(proj.at[:, :, lanes(c)], px.at[c, :, 16 : 16 + TOK], load_sem.at[c])

    def h_load(c):
        return pltpu.make_async_copy(h_hbm.at[:, lanes(c)], hv.at[c], h_sem.at[c])

    mats = [
        pltpu.make_async_copy(a, b, mat_sem.at[i])
        for i, (a, b) in enumerate(zip((m0, m1, m2, m3, m4, m5, m6, m7), (f0, f1, f2, f3, f4, f5, f6, f7)))
    ]
    for c in range(PARTS):
        p_load(c).start()
        h_load(c).start()
    for m in mats:
        m.start()

    def cot_block(c, owner):
        return cot.at[c, pl.ds(pl.multiple_of(owner * 128, 128), 128)]

    def cot_own(c):
        cols = pl.ds(pl.multiple_of(col * CH + c * L, L), L)
        return pltpu.make_async_copy(cot_hbm.at[:, cols], cot_block(c, col), own_sem.at[c])

    def cot_send(c, k):
        peer = lax.rem(col + k, 4)
        cols = pl.ds(pl.multiple_of(peer * CH + c * L, L), L)
        return pltpu.make_async_remote_copy(
            src_ref=cot_hbm.at[:, cols], dst_ref=cot_block(c, col),
            send_sem=a2a_send.at[c, k - 1], recv_sem=a2a_recv.at[c, k - 1], **to_ch(peer))

    def cot_wait(c, k):
        block = cot_block(c, lax.rem(col + 4 - k, 4))
        pltpu.make_async_copy(block, block, a2a_recv.at[c, k - 1]).wait()

    def p_halo(c):
        return pltpu.make_async_remote_copy(
            src_ref=proj.at[:, TOK - 16 : TOK, lanes(c)], dst_ref=px.at[c, :, 0:16],
            send_sem=ph_sem.at[0, c], recv_sem=ph_sem.at[1, c], **to_seq(nxt))

    def gated_halo(c):
        return pltpu.make_async_remote_copy(
            src_ref=gated.at[c, TOK - TAPS : TOK], dst_ref=g_halo.at[c],
            send_sem=gh_sem.at[0, c], recv_sem=gh_sem.at[1, c], **to_seq(nxt))

    def mixed_halo(c):
        return pltpu.make_async_remote_copy(
            src_ref=dm.at[c, 0:TAPS], dst_ref=dm_halo.at[c],
            send_sem=dmh_sem.at[0, c], recv_sem=dmh_sem.at[1, c], **to_seq(prv))

    def grad_halo(c):
        return pltpu.make_async_remote_copy(
            src_ref=ds.at[c, :, 0:16], dst_ref=d_halo.at[c],
            send_sem=dh_sem.at[0, c], recv_sem=dh_sem.at[1, c], **to_seq(prv))

    def gi_store(c):
        return pltpu.make_async_copy(ds.at[c, :, 0:TOK], gi_out.at[:, :, lanes(c)], out_sem.at[c])

    pl.semaphore_wait(barrier, GROUP - 1 + 3 + 3)
    for c in range(PARTS):
        p_halo(c).start()
    for c in range(PARTS):
        cot_own(c).start()
        for k in (2, 1, 3):
            cot_send(c, k).start()

    def stream_block(c, b, l):
        rows = pl.ds(pl.multiple_of(b * 128, 128), 144)
        here = pl.ds(pl.multiple_of(b * 128, 128), 128)
        cols = pl.ds(pl.multiple_of(l * 128, 128), 128)
        wide = pl.ds(pl.multiple_of(c * L + l * 128, 128), 128)
        out = []
        for i, keep in enumerate((qs, ks, vs)):
            x = px[c, i, rows, cols].astype(F32)
            s = sf_ref[i, 0:1, wide] * x[16:144]
            s = s + sf_ref[i, 1:2, wide] * x[15:143]
            s = s + sf_ref[i, 2:3, wide] * x[14:142]
            keep[c, here, cols] = s
            out.append(s)
        gated[c, here, cols] = (out[1] * out[2]).astype(BF16)

    @pl.loop(0, PARTS)
    def _(c):
        p_load(c).wait()

        @pl.loop(0, 3 * LT)
        def _(n):
            stream_block(c, 3 - n // LT, lax.rem(n, LT))

        gated_halo(c).start()
        p_halo(c).wait_recv()

        @pl.when(me == 0)
        def _():
            px[c, :, 0:16] = jnp.zeros((3, 16, L), BF16)

        @pl.loop(0, LT)
        def _(l):
            stream_block(c, 0, l)

    for m in mats:
        m.wait()

    def products(a, b, conj):
        @pl.loop(0, HALF // 16, unroll=2)
        def _(r):
            rows = pl.ds(pl.multiple_of(r * 16, 16), 16)
            rows_i = pl.ds(pl.multiple_of(HALF + r * 16, 16), 16)
            ar, ai, br, bi = a[rows], a[rows_i], b[rows], b[rows_i]
            if conj:
                re, im = ar * br + ai * bi, ai * br - ar * bi
            else:
                re, im = ar * br - ai * bi, ar * bi + ai * br
            for value, start in ((re, 0), (im, HALF)):
                high = value.astype(BF16)
                at = pl.multiple_of(start + r * 16, 16)
                yb[pl.ds(at, 16)] = high
                yb[pl.ds(POINTS + at, 16)] = (value - high.astype(F32)).astype(BF16)

    def back(matrix):
        return dot(matrix[:, : 2 * POINTS], yb[...]) + dot(matrix[:, 2 * POINTS :], yb[0:POINTS])

    def filter_and_mix(c):
        slot, hslot = lax.rem(c, 2), lax.rem(c, 3)
        h_load(c).wait()
        h = hv[c]
        high = h.astype(BF16)
        hb[0:TAPS] = high
        hb[TAPS : 2 * TAPS] = high
        hb[2 * TAPS :] = (h - high.astype(F32)).astype(BF16)
        hhat[hslot] = dot(f4[...], hb[...])
        hhat[hslot, 0:HALF] = hhat[hslot, 0:HALF] + skip_ref[0:1, lanes(c)]
        gated_halo(c).wait_recv()

        @pl.when(me == 0)
        def _():
            g_halo[c] = jnp.zeros((TAPS, L), BF16)

        twice[0:TAPS] = g_halo[c]
        twice[TAPS:] = g_halo[c]
        own = gated[c]
        ghat[slot] = dot(f0[:, TAPS:], own) + dot(f1[:, TAPS:], own) + dot(f2[...], twice[...])
        products(ghat.at[slot], hhat.at[hslot], False)
        mixed[slot] = back(f5)

    def multiply_cotangent(c):
        slot = lax.rem(c, 2)
        cot_own(c).wait()
        for k in (2, 1, 3):
            cot_wait(c, k)

        @pl.loop(0, TOK // 16, unroll=2)
        def _(r):
            rows = pl.ds(pl.multiple_of(r * 16, 16), 16)
            up = cot[c, rows].astype(F32)
            dm[c, rows] = (up * qs[c, rows]).astype(BF16)
            ds[c, 0, rows] = (up * mixed[slot, rows]).astype(BF16)

        mixed_halo(c).start()

    def filter_gradient(c):
        slot = lax.rem(c, 2)
        own = dm[c]
        dhat[slot] = dot(f0[:, :TOK], own) + dot(f1[:, :TOK], own)
        products(ghat.at[slot], dhat.at[slot], True)
        parts[c] = back(f7)

        @pl.loop(1, GROUP)
        def _(k):
            peer = lax.rem(g + k, GROUP)
            pltpu.make_async_remote_copy(
                src_ref=parts.at[c, pl.ds(pl.multiple_of(peer * 8, 8), 8)], dst_ref=landed.at[c, k - 1],
                send_sem=rs_sem.at[0, c], recv_sem=rs_sem.at[1, c], **to_seq(plane + peer)).start()

    def gated_gradient(c):
        slot, hslot = lax.rem(c, 2), lax.rem(c, 3)
        mixed_halo(c).wait_recv()

        @pl.when(me == PEERS - 1)
        def _():
            dm_halo[c] = jnp.zeros((TAPS, L), BF16)

        twice[0:TAPS] = dm_halo[c]
        twice[TAPS:] = dm_halo[c]
        dhat[slot] = dhat[slot] + dot(f3[...], twice[...])
        products(dhat.at[slot], hhat.at[hslot], True)
        grad = back(f6)
        ds[c, 1, 0:TOK] = (grad * vs[c]).astype(BF16)
        ds[c, 2, 0:TOK] = (grad * ks[c]).astype(BF16)
        grad_halo(c).start()

    mine = pl.ds(pl.multiple_of(g * 8, 8), 8)

    def cross(c):
        return pltpu.make_async_remote_copy(
            src_ref=xs.at[c], dst_ref=xr.at[c], send_sem=xx_sem.at[0, c], recv_sem=xx_sem.at[1, c], **to_seq(across))

    def sum_plane(c):
        pltpu.make_async_copy(landed.at[c], landed.at[c], rs_sem.at[1, c]).wait()
        total = parts[c, mine]
        for k in range(GROUP - 1):
            total = total + landed[c, k]
        xs[c] = total
        cross(c).start()

    def spread(c):
        cross(c).wait_recv()
        sums[c, mine] = (xs[c] + xr[c]) * (1.0 / 128.0)

        @pl.loop(1, GROUP)
        def _(k):
            pltpu.make_async_remote_copy(
                src_ref=sums.at[c, mine], dst_ref=sums.at[c, mine],
                send_sem=ag_sem.at[0, c], recv_sem=ag_sem.at[1, c], **to_seq(mate(k))).start()

    def input_gradient(c):
        grad_halo(c).wait()
        ds[c, :, TOK : TOK + 16] = d_halo[c]

        @pl.when(me == PEERS - 1)
        def _():
            ds[c, :, TOK : TOK + 16] = jnp.zeros((3, 16, L), BF16)

        @pl.loop(0, 3 * LT)
        def _(n):
            i, l = n // LT, lax.rem(n, LT)
            cols = pl.ds(pl.multiple_of(l * 128, 128), 128)
            wide = pl.ds(pl.multiple_of(c * L + l * 128, 128), 128)
            acc = [jnp.zeros((8, 128), F32) for _ in range(SHORT)]
            for b in range(4):
                d = ds[c, i, 128 * b : 128 * b + 144, cols].astype(F32)
                p = px[c, i, 16 + 128 * b : 144 + 128 * b, cols].astype(F32)
                result = None
                for j in range(SHORT):
                    moved = d[j : j + 128]
                    term = sf_ref[i, j : j + 1, wide] * moved
                    result = term if result is None else result + term
                    acc[j] = acc[j] + jnp.sum((moved * p).reshape(16, 8, 128), axis=0)
                ds[c, i, 128 * b : 128 * b + 128, cols] = result.astype(BF16)
            for j in range(SHORT):
                gs[c * LT + l, pl.ds(3 * i + j, 1)] = jnp.sum(acc[j], axis=0, keepdims=True)

        gi_store(c).start()

    gs[...] = jnp.zeros(gs.shape, F32)
    filter_and_mix(0)

    @pl.loop(0, PARTS + 2)
    def _(s):
        @pl.when(s < PARTS)
        def _():
            multiply_cotangent(s)
            filter_gradient(s)

        @pl.when(s + 1 < PARTS)
        def _():
            filter_and_mix(s + 1)

        @pl.when(jnp.logical_and(s >= 1, s <= PARTS))
        def _():
            gated_gradient(s - 1)
            sum_plane(s - 1)

        @pl.when(s >= 2)
        def _():
            input_gradient(s - 2)
            spread(s - 2)

    @pl.loop(1, GROUP)
    def _(k):
        peer = lax.rem(g + k, GROUP)
        pltpu.make_async_remote_copy(
            src_ref=gs.at[peer], dst_ref=gs_landed.at[k - 1],
            send_sem=tail_sem.at[0], recv_sem=tail_sem.at[1], **to_seq(plane + peer)).start()

    pltpu.make_async_copy(gs_landed, gs_landed, tail_sem.at[1]).wait()
    total = gs[g]
    for k in range(GROUP - 1):
        total = total + gs_landed[k]
    gs_x[...] = total
    swap = pltpu.make_async_remote_copy(
        src_ref=gs_x, dst_ref=gs_xr, send_sem=tail_sem.at[2], recv_sem=tail_sem.at[3], **to_seq(across))
    swap.start()
    swap.wait()
    gs_sums[g] = (gs_x[...] + gs_xr[...]) * (1.0 / 128.0)

    @pl.loop(1, GROUP)
    def _(k):
        pltpu.make_async_remote_copy(
            src_ref=gs_sums.at[g], dst_ref=gs_sums.at[g],
            send_sem=tail_sem.at[4], recv_sem=tail_sem.at[5], **to_seq(mate(k))).start()

    for c in range(PARTS):
        pltpu.make_async_copy(landed.at[c], landed.at[c], ag_sem.at[1, c]).wait()
        pltpu.make_async_copy(sums.at[c], gl_out.at[:, c * L : c * L + L], h_sem.at[c]).start()
    pltpu.make_async_copy(gs_landed, gs_landed, tail_sem.at[5]).wait()
    for t in range(GROUP):
        gs_out[:, 128 * t : 128 * t + 128] = gs_sums[t]
    pltpu.make_async_copy(gs_landed, gs_landed, tail_sem.at[0]).wait()
    pltpu.make_async_copy(gs_landed, gs_landed, tail_sem.at[4]).wait()
    for c in range(PARTS):
        for k in (2, 1, 3):
            cot_send(c, k).wait_send()
        p_halo(c).wait_send()
        gated_halo(c).wait_send()
        mixed_halo(c).wait_send()
        cross(c).wait_send()
        pltpu.make_async_copy(landed.at[c], landed.at[c], rs_sem.at[0, c]).wait()
        pltpu.make_async_copy(landed.at[c], landed.at[c], ag_sem.at[0, c]).wait()
        gi_store(c).wait()
        pltpu.make_async_copy(sums.at[c], gl_out.at[:, c * L : c * L + L], h_sem.at[c]).wait()


def per_device(projected, short_filters, long_filter, skip_gain, cotangent):
    mats = [jnp.asarray(m) for m in matrices()]
    anywhere = pl.BlockSpec(memory_space=pl.ANY)
    vmem = pl.BlockSpec(memory_space=pltpu.VMEM)
    dma = pltpu.SemaphoreType.DMA
    scratch = [
        pltpu.VMEM((PARTS, 3, TOK + 16, L), BF16),
        pltpu.VMEM((PARTS, TOK, L), F32),
        pltpu.VMEM((PARTS, TOK, L), F32),
        pltpu.VMEM((PARTS, TOK, L), F32),
        pltpu.VMEM((PARTS, TOK, L), BF16),
        pltpu.VMEM((PARTS, TAPS, L), BF16),
        pltpu.VMEM((2, POINTS, L), F32),
        pltpu.VMEM((3, POINTS, L), F32),
        pltpu.VMEM((2, TOK, L), F32),
        pltpu.VMEM((PARTS, TOK, L), BF16),
        pltpu.VMEM((PARTS, TOK, L), BF16),
        pltpu.VMEM((PARTS, TAPS, L), BF16),
        pltpu.VMEM((2, POINTS, L), F32),
        pltpu.VMEM((PARTS, 3, TOK + 16, L), BF16),
        pltpu.VMEM((PARTS, 3, 16, L), BF16),
        pltpu.VMEM((2 * POINTS, L), BF16),
        pltpu.VMEM((3 * TAPS, L), BF16),
        pltpu.VMEM((2 * TAPS, L), BF16),
        pltpu.VMEM((PARTS, TAPS, L), F32),
        *[pltpu.VMEM(m.shape, BF16) for m in mats],
        pltpu.VMEM((PARTS, TAPS, L), F32),
        pltpu.VMEM((PARTS, GROUP - 1, 8, L), F32),
        pltpu.VMEM((PARTS, 8, L), F32),
        pltpu.VMEM((PARTS, 8, L), F32),
        pltpu.VMEM((PARTS, TAPS, L), F32),
        pltpu.VMEM((GROUP, 16, 128), F32),
        pltpu.VMEM((GROUP - 1, 16, 128), F32),
        pltpu.VMEM((16, 128), F32),
        pltpu.VMEM((16, 128), F32),
        pltpu.VMEM((GROUP, 16, 128), F32),
        dma((PARTS,)),
        dma((len(mats),)),
        dma((PARTS,)),
        dma((PARTS,)),
        dma((PARTS,)),
        dma((PARTS, 3)),
        dma((PARTS, 3)),
        *[dma((2, PARTS)) for _ in range(7)],
        dma((6,)),
    ]
    grad_input, grad_long, grad_short = pl.pallas_call(
        kernel,
        out_shape=(
            jax.ShapeDtypeStruct((3, TOK, CH), BF16),
            jax.ShapeDtypeStruct((TAPS, CH), F32),
            jax.ShapeDtypeStruct((16, CH), F32),
        ),
        in_specs=[anywhere, vmem, anywhere, vmem, anywhere] + [anywhere] * len(mats),
        out_specs=(anywhere, anywhere, vmem),
        scratch_shapes=scratch,
        compiler_params=pltpu.CompilerParams(collective_id=0, has_side_effects=True, vmem_limit_bytes=62 << 20),
        cost_estimate=pl.CostEstimate(flops=20 * 10**9, bytes_accessed=24 * 10**6, transcendentals=0),
    )(projected, short_filters, long_filter, skip_gain[None], cotangent, *mats)
    return grad_input, grad_long, grad_long[0], grad_short[:9].reshape(3, SHORT, CH)


def solution(mesh):
    placed = (
        P(None, "seq", "ch"),
        P(None, None, "ch"),
        P(None, "ch"),
        P("ch"),
        P(("seq", "ch"), None),
    )
    return jax.shard_map(
        per_device,
        mesh=mesh,
        in_specs=placed,
        out_specs=(P(None, "seq", "ch"), P(None, "ch"), P("ch"), P(None, None, "ch")),
        check_vma=False,
    )
```

time: 652 us -> 114 us (0.17)
  waiting for transfers between devices: 300 us -> 0 us
  matrix products: 146 us -> 0 us
  Pallas kernels: 0 us -> 103 us
  blocking collectives: 84.4 us -> 0 us
  other arithmetic: 70.4 us -> 0 us
  starting transfers between devices: 15.7 us -> 0 us
  between operations: 14.4 us -> 0.64 us
  local copies, waits for them, and re-layouts: 20.3 us -> 10.7 us
    psum x1 -> x0, waiting for transfers between devices: 288 us -> none  [per_device(): reduced = lax.psum((long_partial, skip_partial, short_partial), 'seq')]
    conv_general_dilated x3 -> x0, matrix products: 146 us -> none  [correlate(): lax.conv_general_dilated(extended[None], kernel[:, None, :], (1,), 'VALID...]
    pallas_call x0 -> x1, Pallas kernels: none -> 103 us  [per_device(): pl.pallas_call(kernel, out_shape=(jax.ShapeDtypeStruct((3, TOK, CH), BF16...]
    psum x1 -> x0, blocking collectives: 84.4 us -> none  [per_device(): reduced = lax.psum((long_partial, skip_partial, short_partial), 'seq')]
    convert_element_type x2 -> x0, other arithmetic: 22.9 us -> none  [the longest x1 14.5 us: per_device(): grad_input.astype(jnp.bfloat16)]
    add x1 -> x0, other arithmetic: 15.9 us -> none  [short_forward(): streams = streams + short_filters[:, offset][:, None, :] * window]
    dot_general x1 -> x0, other arithmetic: 13.8 us -> none  [per_device(): jnp.einsum('itc,itc->ic', stream_grads, own_input[:, short_lag - offset:s...]
    ppermute x4 -> x0, starting transfers between devices: 11.2 us -> none  [passed_along(): lax.ppermute(value, axis, [(source, source + steps) for source in range(i...]
  transfers between devices with their start and end apart: 6 -> 0, of which waited for: 3 -> 0; matrix products, arithmetic and copies ran while one was open for 25% -> 0% of each run, Pallas kernels for 0% -> 0%
where the time goes in v2:
time: 114 us
  Pallas kernels  103 us (90%)
  local copies, waits for them, and re-layouts  10.7 us (9%)
    pallas_call x1, Pallas kernels, per_device(): pl.pallas_call(kernel, out_shape=(jax.ShapeDtypeStruct((3, TOK, CH), BF16...  103 us
    unnamed x4, local copies, waits for them, and re-layouts  7.68 us

profile of v2, /device:TPU:0, one launch (start us, length us, event | category | flops | bytes accessed | tf_op | source)
XLA Modules:
  0.0 114.2 jit_solution(2286805559699883173)
XLA Ops:
  0.6 102.8 %shard_map.156 = (bf16[3,512,2048]{2,1,0:T(8,128)(2,1)}, f32[128,2048]{1,0:T(8,128)}, f32[16,2048]{1,0:T(8,128)}) custom-call(bf16[3,512,2048]{2,1,0:T(8,128)(2,1)} %proj.1, f32[3,3,2048]{2,1,0:T(4,128)} %sf_ref.1, f32[128,2048]{1,0:T(8,128)} %h_hbm.1, f32[1,2048]{1,0:T(1,128)} %bitcast.5, bf16[128,8192]{1,0:T(8,128)(2,1)} %cot_hbm.1, ...), custom_call_target="tpu_custom_call" | custom-call | flops 20000000000 | bytes 24000000 | tf_op jit(solution)/shard_map/pallas_call | solution.py:456
  103.5 1.6 %reshape.11 = f32[3,3,2048]{2,1,0:T(4,128)} reshape(f32[9,2048]{1,0:T(8,128)} %bitcast.3) | data formatting | bytes 147456 | tf_op jit(solution)/shard_map/reshape | solution.py:469
  105.1 1.4 %slice.6 = f32[1,2048]{1,0:T(1,128)} slice(f32[128,2048]{1,0:T(8,128)} %get-tuple-element.15), slice={[0:1], [0:2048]} | slice | bytes 16384 | tf_op jit(solution)/shard_map/slice | solution.py:469
  106.5 0.0 copy-start
  106.5 6.7 %copy.19 = bf16[3,512,2048]{2,1,0:T(8,128)(2,1)} copy(bf16[3,512,2048]{2,1,0:T(8,128)(2,1)} %get-tuple-element.14) | data formatting | bytes 12582912
  113.2 0.0 copy-done
  113.2 1.0 copy.20
Async XLA Ops:
  106.5 6.7 %copy-start = (f32[128,2048]{1,0:T(8,128)S(1)}, f32[128,2048]{1,0:T(8,128)}, u32[]{:S(2)}) copy-start(f32[128,2048]{1,0:T(8,128)} %get-tuple-element.15) | copy-start | bytes 3145732

commit v3 on v2

--- a/solution.py
+++ b/solution.py
@@ -59,11 +59,11 @@
 
 def kernel(
     proj, sf_ref, h_hbm, skip_ref, cot_hbm, m0, m1, m2, m3, m4, m5, m6, m7,
-    gi_out, gl_out, gs_out,
-    px, qs, ks, vs, gated, g_halo, ghat, hhat, mixed, cot, dm, dm_halo, dhat, ds, d_halo,
+    d_out, gl_out, gs_out,
+    px, tip, p_halo_ref, qs, ks, vs, gated, g_halo, ghat, hhat, mixed, cot, dm, dm_halo, dhat, ds, d_halo,
     yb, hb, twice, hv, f0, f1, f2, f3, f4, f5, f6, f7,
-    parts, landed, xs, xr, sums, gs, gs_landed, gs_x, gs_xr, gs_sums,
-    load_sem, mat_sem, h_sem, own_sem, out_sem, a2a_send, a2a_recv,
+    parts, landed, xs, xr, sums, gs, gs_landed, gs_sums,
+    load_sem, mat_sem, h_sem, own_sem, out_sem, halo_out_sem, a2a_send, a2a_recv,
     ph_sem, gh_sem, dmh_sem, dh_sem, rs_sem, xx_sem, ag_sem, tail_sem,
 ):
     me = lax.axis_index("seq")
@@ -83,12 +83,10 @@
     def mate(k):
         return plane + lax.rem(g + k, GROUP)
 
-    @pl.loop(1, GROUP)
+    @pl.loop(1, PEERS)
     def _(k):
-        pl.semaphore_signal(barrier, inc=1, **to_seq(mate(k)))
-
-    for s in (nxt, prv, across):
-        pl.semaphore_signal(barrier, inc=1, **to_seq(s))
+        pl.semaphore_signal(barrier, inc=1, **to_seq(lax.rem(me + k, PEERS)))
+
     for k in range(1, 4):
         pl.semaphore_signal(barrier, inc=1, **to_ch(lax.rem(col + k, 4)))
 
@@ -131,7 +129,7 @@
 
     def p_halo(c):
         return pltpu.make_async_remote_copy(
-            src_ref=proj.at[:, TOK - 16 : TOK, lanes(c)], dst_ref=px.at[c, :, 0:16],
+            src_ref=tip.at[c], dst_ref=p_halo_ref.at[c],
             send_sem=ph_sem.at[0, c], recv_sem=ph_sem.at[1, c], **to_seq(nxt))
 
     def gated_halo(c):
@@ -149,16 +147,21 @@
             src_ref=ds.at[c, :, 0:16], dst_ref=d_halo.at[c],
             send_sem=dh_sem.at[0, c], recv_sem=dh_sem.at[1, c], **to_seq(prv))
 
-    def gi_store(c):
-        return pltpu.make_async_copy(ds.at[c, :, 0:TOK], gi_out.at[:, :, lanes(c)], out_sem.at[c])
-
-    pl.semaphore_wait(barrier, GROUP - 1 + 3 + 3)
-    for c in range(PARTS):
-        p_halo(c).start()
-    for c in range(PARTS):
+    def d_store(c):
+        return pltpu.make_async_copy(ds.at[c, :, 0:TOK], d_out.at[:, 0:TOK, lanes(c)], out_sem.at[c])
+
+    def halo_store(c):
+        return pltpu.make_async_copy(d_halo.at[c], d_out.at[:, TOK : TOK + 16, lanes(c)], halo_out_sem.at[c])
+
+    def cot_start(c):
         cot_own(c).start()
         for k in (2, 1, 3):
             cot_send(c, k).start()
+
+    has_next, has_previous = me < PEERS - 1, me > 0
+
+    pl.semaphore_wait(barrier, PEERS - 1 + 3)
+    cot_start(0)
 
     def stream_block(c, b, l):
         rows = pl.ds(pl.multiple_of(b * 128, 128), 144)
@@ -178,17 +181,39 @@
     @pl.loop(0, PARTS)
     def _(c):
         p_load(c).wait()
-
+        last = [px[c, i, TOK : TOK + 16].astype(F32)[14:16] for i in range(3)]
+        tip[c] = jnp.concatenate(last + [jnp.zeros((10, L), F32)], axis=0).astype(BF16)
+
+        @pl.when(has_next)
+        def _():
+            p_halo(c).start()
+
+    @pl.loop(0, PARTS)
+    def _(c):
         @pl.loop(0, 3 * LT)
         def _(n):
             stream_block(c, 3 - n // LT, lax.rem(n, LT))
 
-        gated_halo(c).start()
-        p_halo(c).wait_recv()
+        @pl.when(has_next)
+        def _():
+            gated_halo(c).start()
+
+    cot_start(1)
+
+    @pl.loop(0, PARTS)
+    def _(c):
+        @pl.when(has_previous)
+        def _():
+            p_halo(c).wait_recv()
 
         @pl.when(me == 0)
         def _():
-            px[c, :, 0:16] = jnp.zeros((3, 16, L), BF16)
+            p_halo_ref[c] = jnp.zeros((16, L), BF16)
+
+        before = p_halo_ref[c].astype(F32)
+        for i in range(3):
+            rows = jnp.concatenate([jnp.zeros((14, L), F32), before[2 * i : 2 * i + 2]], axis=0)
+            px[c, i, 0:16] = rows.astype(BF16)
 
         @pl.loop(0, LT)
         def _(l):
@@ -226,7 +251,9 @@
         hb[2 * TAPS :] = (h - high.astype(F32)).astype(BF16)
         hhat[hslot] = dot(f4[...], hb[...])
         hhat[hslot, 0:HALF] = hhat[hslot, 0:HALF] + skip_ref[0:1, lanes(c)]
-        gated_halo(c).wait_recv()
+        @pl.when(has_previous)
+        def _():
+            gated_halo(c).wait_recv()
 
         @pl.when(me == 0)
         def _():
@@ -252,7 +279,9 @@
             dm[c, rows] = (up * qs[c, rows]).astype(BF16)
             ds[c, 0, rows] = (up * mixed[slot, rows]).astype(BF16)
 
-        mixed_halo(c).start()
+        @pl.when(has_previous)
+        def _():
+            mixed_halo(c).start()
 
     def filter_gradient(c):
         slot = lax.rem(c, 2)
@@ -270,7 +299,9 @@
 
     def gated_gradient(c):
         slot, hslot = lax.rem(c, 2), lax.rem(c, 3)
-        mixed_halo(c).wait_recv()
+        @pl.when(has_next)
+        def _():
+            mixed_halo(c).wait_recv()
 
         @pl.when(me == PEERS - 1)
         def _():
@@ -283,7 +314,11 @@
         grad = back(f6)
         ds[c, 1, 0:TOK] = (grad * vs[c]).astype(BF16)
         ds[c, 2, 0:TOK] = (grad * ks[c]).astype(BF16)
-        grad_halo(c).start()
+        d_store(c).start()
+
+        @pl.when(has_previous)
+        def _():
+            grad_halo(c).start()
 
     mine = pl.ds(pl.multiple_of(g * 8, 8), 8)
 
@@ -309,40 +344,40 @@
                 src_ref=sums.at[c, mine], dst_ref=sums.at[c, mine],
                 send_sem=ag_sem.at[0, c], recv_sem=ag_sem.at[1, c], **to_seq(mate(k))).start()
 
-    def input_gradient(c):
-        grad_halo(c).wait()
+    def short_gradient(c):
+        @pl.when(has_next)
+        def _():
+            grad_halo(c).wait_recv()
+
+        @pl.when(me == PEERS - 1)
+        def _():
+            d_halo[c] = jnp.zeros((3, 16, L), BF16)
+
+        halo_store(c).start()
         ds[c, :, TOK : TOK + 16] = d_halo[c]
-
-        @pl.when(me == PEERS - 1)
-        def _():
-            ds[c, :, TOK : TOK + 16] = jnp.zeros((3, 16, L), BF16)
 
         @pl.loop(0, 3 * LT)
         def _(n):
             i, l = n // LT, lax.rem(n, LT)
             cols = pl.ds(pl.multiple_of(l * 128, 128), 128)
-            wide = pl.ds(pl.multiple_of(c * L + l * 128, 128), 128)
             acc = [jnp.zeros((8, 128), F32) for _ in range(SHORT)]
             for b in range(4):
                 d = ds[c, i, 128 * b : 128 * b + 144, cols].astype(F32)
                 p = px[c, i, 16 + 128 * b : 144 + 128 * b, cols].astype(F32)
-                result = None
                 for j in range(SHORT):
-                    moved = d[j : j + 128]
-                    term = sf_ref[i, j : j + 1, wide] * moved
-                    result = term if result is None else result + term
-                    acc[j] = acc[j] + jnp.sum((moved * p).reshape(16, 8, 128), axis=0)
-                ds[c, i, 128 * b : 128 * b + 128, cols] = result.astype(BF16)
+                    acc[j] = acc[j] + jnp.sum((d[j : j + 128] * p).reshape(16, 8, 128), axis=0)
             for j in range(SHORT):
                 gs[c * LT + l, pl.ds(3 * i + j, 1)] = jnp.sum(acc[j], axis=0, keepdims=True)
 
-        gi_store(c).start()
-
     gs[...] = jnp.zeros(gs.shape, F32)
     filter_and_mix(0)
 
     @pl.loop(0, PARTS + 2)
     def _(s):
+        @pl.when(s + 2 < PARTS)
+        def _():
+            cot_start(s + 2)
+
         @pl.when(s < PARTS)
         def _():
             multiply_cotangent(s)
@@ -359,52 +394,119 @@
 
         @pl.when(s >= 2)
         def _():
-            input_gradient(s - 2)
             spread(s - 2)
-
-    @pl.loop(1, GROUP)
+            short_gradient(s - 2)
+
+    @pl.loop(1, PEERS)
     def _(k):
-        peer = lax.rem(g + k, GROUP)
+        peer = lax.rem(me + k, PEERS)
         pltpu.make_async_remote_copy(
-            src_ref=gs.at[peer], dst_ref=gs_landed.at[k - 1],
-            send_sem=tail_sem.at[0], recv_sem=tail_sem.at[1], **to_seq(plane + peer)).start()
-
-    pltpu.make_async_copy(gs_landed, gs_landed, tail_sem.at[1]).wait()
-    total = gs[g]
-    for k in range(GROUP - 1):
+            src_ref=gs.at[lax.rem(peer, GROUP)], dst_ref=gs_landed.at[me],
+            send_sem=tail_sem.at[0], recv_sem=tail_sem.at[1], **to_seq(peer)).start()
+
+    gs_landed[me] = gs[g]
+    others = gs_landed.at[0 : PEERS - 1]
+    mates = gs_landed.at[0 : GROUP - 1]
+    pltpu.make_async_copy(others, others, tail_sem.at[1]).wait()
+    total = gs_landed[0]
+    for k in range(1, PEERS):
         total = total + gs_landed[k]
-    gs_x[...] = total
-    swap = pltpu.make_async_remote_copy(
-        src_ref=gs_x, dst_ref=gs_xr, send_sem=tail_sem.at[2], recv_sem=tail_sem.at[3], **to_seq(across))
-    swap.start()
-    swap.wait()
-    gs_sums[g] = (gs_x[...] + gs_xr[...]) * (1.0 / 128.0)
+    gs_sums[g] = total * (1.0 / 128.0)
 
     @pl.loop(1, GROUP)
     def _(k):
         pltpu.make_async_remote_copy(
             src_ref=gs_sums.at[g], dst_ref=gs_sums.at[g],
-            send_sem=tail_sem.at[4], recv_sem=tail_sem.at[5], **to_seq(mate(k))).start()
-
-    for c in range(PARTS):
+            send_sem=tail_sem.at[2], recv_sem=tail_sem.at[3], **to_seq(mate(k))).start()
+
+    def gl_store(c):
+        return pltpu.make_async_copy(sums.at[c], gl_out.at[:, lanes(c)], h_sem.at[c])
+
+    @pl.loop(0, PARTS)
+    def _(c):
         pltpu.make_async_copy(landed.at[c], landed.at[c], ag_sem.at[1, c]).wait()
-        pltpu.make_async_copy(sums.at[c], gl_out.at[:, c * L : c * L + L], h_sem.at[c]).start()
-    pltpu.make_async_copy(gs_landed, gs_landed, tail_sem.at[5]).wait()
-    for t in range(GROUP):
-        gs_out[:, 128 * t : 128 * t + 128] = gs_sums[t]
-    pltpu.make_async_copy(gs_landed, gs_landed, tail_sem.at[0]).wait()
-    pltpu.make_async_copy(gs_landed, gs_landed, tail_sem.at[4]).wait()
-    for c in range(PARTS):
+        gl_store(c).start()
         for k in (2, 1, 3):
             cot_send(c, k).wait_send()
-        p_halo(c).wait_send()
-        gated_halo(c).wait_send()
-        mixed_halo(c).wait_send()
+
+        @pl.when(has_next)
+        def _():
+            p_halo(c).wait_send()
+            gated_halo(c).wait_send()
+
+        @pl.when(has_previous)
+        def _():
+            mixed_halo(c).wait_send()
+            grad_halo(c).wait_send()
+
         cross(c).wait_send()
         pltpu.make_async_copy(landed.at[c], landed.at[c], rs_sem.at[0, c]).wait()
         pltpu.make_async_copy(landed.at[c], landed.at[c], ag_sem.at[0, c]).wait()
-        gi_store(c).wait()
-        pltpu.make_async_copy(sums.at[c], gl_out.at[:, c * L : c * L + L], h_sem.at[c]).wait()
+        d_store(c).wait()
+        halo_store(c).wait()
+        gl_store(c).wait()
+
+    pltpu.make_async_copy(others, others, tail_sem.at[0]).wait()
+    pltpu.make_async_copy(mates, mates, tail_sem.at[3]).wait()
+    pltpu.make_async_copy(mates, mates, tail_sem.at[2]).wait()
+    gs_out[...] = gs_sums[...]
+
+
+def finish_kernel(sf_ref, d_ref, gl_ref, top_ref, gs_ref, gi_out, gl_out, skip_out, gs_out):
+    c, i = pl.program_id(0), pl.program_id(1)
+
+    @pl.loop(0, 4 * LT)
+    def _(n):
+        l, b = n // 4, lax.rem(n, 4)
+        cols = pl.ds(pl.multiple_of(l * 128, 128), 128)
+        wide = pl.ds(pl.multiple_of(c * L + l * 128, 128), 128)
+        d = d_ref[0, pl.ds(pl.multiple_of(b * 128, 128), 144), cols].astype(F32)
+        result = sf_ref[i, 0:1, wide] * d[0:128]
+        for j in range(1, SHORT):
+            result = result + sf_ref[i, j : j + 1, wide] * d[j : j + 128]
+        gi_out[0, pl.ds(pl.multiple_of(b * 128, 128), 128), cols] = result.astype(BF16)
+
+    @pl.when(i == 0)
+    def _():
+        gl_out[...] = gl_ref[...]
+
+    @pl.when(jnp.logical_and(c == 0, i == 0))
+    def _():
+        skip_out[...] = top_ref[0]
+        for stream in range(3):
+            for j in range(SHORT):
+                row = 3 * stream + j
+                gs_out[stream, j : j + 1] = jnp.concatenate(
+                    [gs_ref[t, row : row + 1] for t in range(GROUP)], axis=1)
+
+
+def finish(short_filters, d, gl, gs):
+    whole = lambda shape: pl.BlockSpec(shape, lambda c, i: (0,) * len(shape))
+    return pl.pallas_call(
+        finish_kernel,
+        grid=(PARTS, 3),
+        out_shape=(
+            jax.ShapeDtypeStruct((3, TOK, CH), BF16),
+            jax.ShapeDtypeStruct((TAPS, CH), F32),
+            jax.ShapeDtypeStruct((CH,), F32),
+            jax.ShapeDtypeStruct((3, SHORT, CH), F32),
+        ),
+        in_specs=[
+            whole((3, SHORT, CH)),
+            pl.BlockSpec((1, TOK + 16, L), lambda c, i: (i, 0, c)),
+            pl.BlockSpec((TAPS, L), lambda c, i: (0, c)),
+            whole((8, CH)),
+            whole((GROUP, 16, 128)),
+        ],
+        out_specs=(
+            pl.BlockSpec((1, TOK, L), lambda c, i: (i, 0, c)),
+            pl.BlockSpec((TAPS, L), lambda c, i: (0, c)),
+            whole((CH,)),
+            whole((3, SHORT, CH)),
+        ),
+        compiler_params=pltpu.CompilerParams(vmem_limit_bytes=24 << 20),
+        cost_estimate=pl.CostEstimate(flops=2 * 10**7, bytes_accessed=16 * 10**6, transcendentals=0),
+    )(short_filters, d, gl, gl, gs)
 
 
 def per_device(projected, short_filters, long_filter, skip_gain, cotangent):
@@ -414,6 +516,8 @@
     dma = pltpu.SemaphoreType.DMA
     scratch = [
         pltpu.VMEM((PARTS, 3, TOK + 16, L), BF16),
+        pltpu.VMEM((PARTS, 16, L), BF16),
+        pltpu.VMEM((PARTS, 16, L), BF16),
         pltpu.VMEM((PARTS, TOK, L), F32),
         pltpu.VMEM((PARTS, TOK, L), F32),
         pltpu.VMEM((PARTS, TOK, L), F32),
@@ -439,26 +543,25 @@
         pltpu.VMEM((PARTS, 8, L), F32),
         pltpu.VMEM((PARTS, TAPS, L), F32),
         pltpu.VMEM((GROUP, 16, 128), F32),
-        pltpu.VMEM((GROUP - 1, 16, 128), F32),
-        pltpu.VMEM((16, 128), F32),
-        pltpu.VMEM((16, 128), F32),
+        pltpu.VMEM((PEERS, 16, 128), F32),
         pltpu.VMEM((GROUP, 16, 128), F32),
         dma((PARTS,)),
         dma((len(mats),)),
         dma((PARTS,)),
         dma((PARTS,)),
         dma((PARTS,)),
+        dma((PARTS,)),
         dma((PARTS, 3)),
         dma((PARTS, 3)),
         *[dma((2, PARTS)) for _ in range(7)],
-        dma((6,)),
+        dma((4,)),
     ]
-    grad_input, grad_long, grad_short = pl.pallas_call(
+    d, gl, gs = pl.pallas_call(
         kernel,
         out_shape=(
-            jax.ShapeDtypeStruct((3, TOK, CH), BF16),
+            jax.ShapeDtypeStruct((3, TOK + 16, CH), BF16),
             jax.ShapeDtypeStruct((TAPS, CH), F32),
-            jax.ShapeDtypeStruct((16, CH), F32),
+            jax.ShapeDtypeStruct((GROUP, 16, 128), F32),
         ),
         in_specs=[anywhere, vmem, anywhere, vmem, anywhere] + [anywhere] * len(mats),
         out_specs=(anywhere, anywhere, vmem),
@@ -466,7 +569,7 @@
         compiler_params=pltpu.CompilerParams(collective_id=0, has_side_effects=True, vmem_limit_bytes=62 << 20),
         cost_estimate=pl.CostEstimate(flops=20 * 10**9, bytes_accessed=24 * 10**6, transcendentals=0),
     )(projected, short_filters, long_filter, skip_gain[None], cotangent, *mats)
-    return grad_input, grad_long, grad_long[0], grad_short[:9].reshape(3, SHORT, CH)
+    return finish(short_filters, d, gl, gs)
 
 
 def solution(mesh):

time: 114 us -> 101 us (0.89)
  the two profiles are of different devices: /device:TPU:0 before, /device:TPU:6 now
where the time goes in v3:
time: 101 us; the launch traced here: 100 us
  Pallas kernels  94.7 us (94%)
  local copies, waits for them, and re-layouts  4.97 us (5%)
    pallas_call x1, Pallas kernels, per_device(): pl.pallas_call(kernel, out_shape=(jax.ShapeDtypeStruct((3, TOK + 16, CH),...  84.6 us
    pallas_call x1, Pallas kernels, finish(): pl.pallas_call(finish_kernel, grid=(PARTS, 3), out_shape=(jax.ShapeDtypeS...  10 us
    unnamed x8, local copies, waits for them, and re-layouts  4.97 us

profile of v3, /device:TPU:6, one launch (start us, length us, event | category | flops | bytes accessed | tf_op | source)
XLA Modules:
  0.0 100.3 jit_solution(330133697253601)
XLA Ops:
  0.6 0.0 copy-start.3
  0.6 84.6 %shard_map.156 = (bf16[3,528,2048]{2,1,0:T(8,128)(2,1)}, f32[128,2048]{1,0:T(8,128)}, f32[16,16,128]{2,1,0:T(8,128)}) custom-call(bf16[3,512,2048]{2,1,0:T(8,128)(2,1)} %proj.1, f32[3,3,2048]{2,1,0:T(4,128)} %sf_ref.3, f32[128,2048]{1,0:T(8,128)} %h_hbm.1, f32[1,2048]{1,0:T(1,128)} %bitcast.1, bf16[128,8192]{1,0:T(8,128)(2,1)} %cot_hbm.1, ...), custom_call_target="tpu_custom_call" | custom-call | flops 20000000000 | bytes 24000000 | tf_op jit(solution)/shard_map/pallas_call | solution.py:559
  85.3 0.0 copy-done.3
  85.3 0.0 copy-start
  85.3 2.8 %copy-done = bf16[3,528,2048]{2,1,0:T(8,128)(2,1)S(1)} copy-done((bf16[3,528,2048]{2,1,0:T(8,128)(2,1)S(1)}, bf16[3,528,2048]{2,1,0:T(8,128)(2,1)}, u32[]{:S(2)}) %copy-start) | copy-done | bytes 6488088
  88.1 0.0 copy-start.1
  88.1 1.2 %copy-done.1 = f32[128,2048]{1,0:T(8,128)S(1)} copy-done((f32[128,2048]{1,0:T(8,128)S(1)}, f32[128,2048]{1,0:T(8,128)}, u32[]{:S(2)}) %copy-start.1) | copy-done | bytes 1048600
  89.4 0.0 copy-start.2
  89.4 0.9 copy-done.2
  90.3 10.0 %shard_map.157 = (bf16[3,512,2048]{2,1,0:T(8,128)(2,1)}, f32[128,2048]{1,0:T(8,128)}, f32[2048]{0:T(1024)}, f32[3,3,2048]{2,1,0:T(4,128)}) custom-call(f32[3,3,2048]{2,1,0:T(4,128)S(1)} %copy-done.3, bf16[3,528,2048]{2,1,0:T(8,128)(2,1)S(1)} %copy-done, f32[128,2048]{1,0:T(8,128)S(1)} %copy-done.1, f32[128,2048]{1,0:T(8,128)S(1)} %copy-done.1, ...), custom_call_target="tpu_custom_call" | custom-call | flops 20000000 | bytes 16000000 | tf_op jit(solution)/shard_map/pallas_call | solution.py:485
Async XLA Ops:
  0.6 84.7 %copy-start.3 = (f32[3,3,2048]{2,1,0:T(4,128)S(1)}, f32[3,3,2048]{2,1,0:T(4,128)}, u32[]{:S(2)}) copy-start(f32[3,3,2048]{2,1,0:T(4,128)} %sf_ref.3) | copy-start | bytes 221188
  85.3 2.8 %copy-start = (bf16[3,528,2048]{2,1,0:T(8,128)(2,1)S(1)}, bf16[3,528,2048]{2,1,0:T(8,128)(2,1)}, u32[]{:S(2)}) copy-start(bf16[3,528,2048]{2,1,0:T(8,128)(2,1)} %get-tuple-element.7.d_ref) | copy-start | bytes 19464196
  88.1 1.2 %copy-start.1 = (f32[128,2048]{1,0:T(8,128)S(1)}, f32[128,2048]{1,0:T(8,128)}, u32[]{:S(2)}) copy-start(f32[128,2048]{1,0:T(8,128)} %get-tuple-element.8.gl_ref.top_ref) | copy-start | bytes 3145732
  89.4 0.9 copy-start.2

commit v4 on v3

--- a/solution.py
+++ b/solution.py
@@ -61,7 +61,7 @@
     proj, sf_ref, h_hbm, skip_ref, cot_hbm, m0, m1, m2, m3, m4, m5, m6, m7,
     d_out, gl_out, gs_out,
     px, tip, p_halo_ref, qs, ks, vs, gated, g_halo, ghat, hhat, mixed, cot, dm, dm_halo, dhat, ds, d_halo,
-    yb, hb, twice, hv, f0, f1, f2, f3, f4, f5, f6, f7,
+    yb, hb, twice, line, hv, f0, f1, f2, f3, f4, f5, f6, f7,
     parts, landed, xs, xr, sums, gs, gs_landed, gs_sums,
     load_sem, mat_sem, h_sem, own_sem, out_sem, halo_out_sem, a2a_send, a2a_recv,
     ph_sem, gh_sem, dmh_sem, dh_sem, rs_sem, xx_sem, ag_sem, tail_sem,
@@ -160,27 +160,32 @@
 
     has_next, has_previous = me < PEERS - 1, me > 0
 
+    def stream_rows(c, l):
+        cols = pl.ds(pl.multiple_of(l * 128, 128), 128)
+        wide = pl.ds(pl.multiple_of(c * L + l * 128, 128), 128)
+        for i in range(3):
+            line[i] = px[c, i, :, cols].astype(F32)
+        taps = [[sf_ref[i, j : j + 1, wide] for j in range(SHORT)] for i in range(3)]
+
+        @pl.loop(0, TOK // 64, unroll=4)
+        def _(b):
+            here = pl.ds(pl.multiple_of(b * 64, 64), 64)
+            out = []
+            for i, keep in enumerate((qs, ks, vs)):
+                s = taps[i][0] * line[i, pl.ds(b * 64 + 16, 64)]
+                s = s + taps[i][1] * line[i, pl.ds(b * 64 + 15, 64)]
+                s = s + taps[i][2] * line[i, pl.ds(b * 64 + 14, 64)]
+                keep[c, here, cols] = s
+                out.append(s)
+            gated[c, here, cols] = (out[1] * out[2]).astype(BF16)
+
     pl.semaphore_wait(barrier, PEERS - 1 + 3)
     cot_start(0)
-
-    def stream_block(c, b, l):
-        rows = pl.ds(pl.multiple_of(b * 128, 128), 144)
-        here = pl.ds(pl.multiple_of(b * 128, 128), 128)
-        cols = pl.ds(pl.multiple_of(l * 128, 128), 128)
-        wide = pl.ds(pl.multiple_of(c * L + l * 128, 128), 128)
-        out = []
-        for i, keep in enumerate((qs, ks, vs)):
-            x = px[c, i, rows, cols].astype(F32)
-            s = sf_ref[i, 0:1, wide] * x[16:144]
-            s = s + sf_ref[i, 1:2, wide] * x[15:143]
-            s = s + sf_ref[i, 2:3, wide] * x[14:142]
-            keep[c, here, cols] = s
-            out.append(s)
-        gated[c, here, cols] = (out[1] * out[2]).astype(BF16)
 
     @pl.loop(0, PARTS)
     def _(c):
         p_load(c).wait()
+        px[c, :, 0:16] = jnp.zeros((3, 16, L), BF16)
         last = [px[c, i, TOK : TOK + 16].astype(F32)[14:16] for i in range(3)]
         tip[c] = jnp.concatenate(last + [jnp.zeros((10, L), F32)], axis=0).astype(BF16)
 
@@ -188,17 +193,34 @@
         def _():
             p_halo(c).start()
 
-    @pl.loop(0, PARTS)
-    def _(c):
-        @pl.loop(0, 3 * LT)
-        def _(n):
-            stream_block(c, 3 - n // LT, lax.rem(n, LT))
-
-        @pl.when(has_next)
+        @pl.loop(0, LT)
+        def _(l):
+            stream_rows(c, l)
+
+        @pl.when(jnp.logical_and(has_next, c == 0))
         def _():
             gated_halo(c).start()
 
+    @pl.when(has_next)
+    def _():
+        gated_halo(1).start()
+
     cot_start(1)
+    for m in mats:
+        m.wait()
+
+    def filter_transform(c):
+        h_load(c).wait()
+        h = hv[c]
+        high = h.astype(BF16)
+        hb[0:TAPS] = high
+        hb[TAPS : 2 * TAPS] = high
+        hb[2 * TAPS :] = (h - high.astype(F32)).astype(BF16)
+        hslot = lax.rem(c, 3)
+        hhat[hslot] = dot(f4[...], hb[...])
+        hhat[hslot, 0:HALF] = hhat[hslot, 0:HALF] + skip_ref[0:1, lanes(c)]
+
+    filter_transform(0)
 
     @pl.loop(0, PARTS)
     def _(c):
@@ -211,16 +233,15 @@
             p_halo_ref[c] = jnp.zeros((16, L), BF16)
 
         before = p_halo_ref[c].astype(F32)
-        for i in range(3):
-            rows = jnp.concatenate([jnp.zeros((14, L), F32), before[2 * i : 2 * i + 2]], axis=0)
-            px[c, i, 0:16] = rows.astype(BF16)
-
-        @pl.loop(0, LT)
-        def _(l):
-            stream_block(c, 0, l)
-
-    for m in mats:
-        m.wait()
+        out = []
+        for i, keep in enumerate((qs, ks, vs)):
+            x = jnp.concatenate([before[2 * i : 2 * i + 2], px[c, i, 16:32].astype(F32)], axis=0)
+            s = sf_ref[i, 0:1, lanes(c)] * x[2:18]
+            s = s + sf_ref[i, 1:2, lanes(c)] * x[1:17]
+            s = s + sf_ref[i, 2:3, lanes(c)] * x[0:16]
+            keep[c, 0:16] = s
+            out.append(s)
+        gated[c, 0:16] = (out[1] * out[2]).astype(BF16)
 
     def products(a, b, conj):
         @pl.loop(0, HALF // 16, unroll=2)
@@ -243,14 +264,9 @@
 
     def filter_and_mix(c):
         slot, hslot = lax.rem(c, 2), lax.rem(c, 3)
-        h_load(c).wait()
-        h = hv[c]
-        high = h.astype(BF16)
-        hb[0:TAPS] = high
-        hb[TAPS : 2 * TAPS] = high
-        hb[2 * TAPS :] = (h - high.astype(F32)).astype(BF16)
-        hhat[hslot] = dot(f4[...], hb[...])
-        hhat[hslot, 0:HALF] = hhat[hslot, 0:HALF] + skip_ref[0:1, lanes(c)]
+        own = gated[c]
+        ghat[slot] = dot(f0[:, TAPS:], own) + dot(f1[:, TAPS:], own)
+
         @pl.when(has_previous)
         def _():
             gated_halo(c).wait_recv()
@@ -261,8 +277,7 @@
 
         twice[0:TAPS] = g_halo[c]
         twice[TAPS:] = g_halo[c]
-        own = gated[c]
-        ghat[slot] = dot(f0[:, TAPS:], own) + dot(f1[:, TAPS:], own) + dot(f2[...], twice[...])
+        ghat[slot] = ghat[slot] + dot(f2[...], twice[...])
         products(ghat.at[slot], hhat.at[hslot], False)
         mixed[slot] = back(f5)
 
@@ -360,49 +375,78 @@
         def _(n):
             i, l = n // LT, lax.rem(n, LT)
             cols = pl.ds(pl.multiple_of(l * 128, 128), 128)
-            acc = [jnp.zeros((8, 128), F32) for _ in range(SHORT)]
-            for b in range(4):
-                d = ds[c, i, 128 * b : 128 * b + 144, cols].astype(F32)
-                p = px[c, i, 16 + 128 * b : 144 + 128 * b, cols].astype(F32)
-                for j in range(SHORT):
-                    acc[j] = acc[j] + jnp.sum((d[j : j + 128] * p).reshape(16, 8, 128), axis=0)
+            line[i] = ds[c, i, :, cols].astype(F32)
+
+            def rows(b, acc):
+                p = px[c, i, pl.ds(pl.multiple_of(16 + b * 64, 16), 64), cols].astype(F32)
+                return tuple(
+                    acc[j] + jnp.sum((line[i, pl.ds(b * 64 + j, 64)] * p).reshape(8, 8, 128), axis=0)
+                    for j in range(SHORT))
+
+            acc = lax.fori_loop(0, TOK // 64, rows, tuple(jnp.zeros((8, 128), F32) for _ in range(SHORT)), unroll=8)
             for j in range(SHORT):
                 gs[c * LT + l, pl.ds(3 * i + j, 1)] = jnp.sum(acc[j], axis=0, keepdims=True)
 
+        @pl.loop(0, 2 * LT)
+        def _(n):
+            owner = c * LT + lax.rem(n, LT)
+            peer = owner + GROUP * (n // LT)
+
+            @pl.when(peer != me)
+            def _():
+                pltpu.make_async_remote_copy(
+                    src_ref=gs.at[owner], dst_ref=gs_landed.at[me],
+                    send_sem=tail_sem.at[0], recv_sem=tail_sem.at[1], **to_seq(peer)).start()
+
     gs[...] = jnp.zeros(gs.shape, F32)
     filter_and_mix(0)
 
     @pl.loop(0, PARTS + 2)
     def _(s):
+        @pl.when(s < PARTS)
+        def _():
+            multiply_cotangent(s)
+
         @pl.when(s + 2 < PARTS)
         def _():
+            @pl.when(has_next)
+            def _():
+                gated_halo(s + 2).start()
+
             cot_start(s + 2)
 
         @pl.when(s < PARTS)
         def _():
-            multiply_cotangent(s)
             filter_gradient(s)
 
         @pl.when(s + 1 < PARTS)
         def _():
+            filter_transform(s + 1)
             filter_and_mix(s + 1)
 
+        @pl.when(jnp.logical_and(s >= 2, s <= PARTS))
+        def _():
+            sum_plane(s - 2)
+
         @pl.when(jnp.logical_and(s >= 1, s <= PARTS))
         def _():
             gated_gradient(s - 1)
-            sum_plane(s - 1)
+
+        @pl.when(jnp.logical_and(s >= 2, s <= PARTS))
+        def _():
+            spread(s - 2)
+
+        @pl.when(s == PARTS)
+        def _():
+            sum_plane(PARTS - 1)
+
+        @pl.when(s == PARTS + 1)
+        def _():
+            spread(PARTS - 1)
 
         @pl.when(s >= 2)
         def _():
-            spread(s - 2)
             short_gradient(s - 2)
-
-    @pl.loop(1, PEERS)
-    def _(k):
-        peer = lax.rem(me + k, PEERS)
-        pltpu.make_async_remote_copy(
-            src_ref=gs.at[lax.rem(peer, GROUP)], dst_ref=gs_landed.at[me],
-            send_sem=tail_sem.at[0], recv_sem=tail_sem.at[1], **to_seq(peer)).start()
 
     gs_landed[me] = gs[g]
     others = gs_landed.at[0 : PEERS - 1]
@@ -452,27 +496,36 @@
     gs_out[...] = gs_sums[...]
 
 
-def finish_kernel(sf_ref, d_ref, gl_ref, top_ref, gs_ref, gi_out, gl_out, skip_out, gs_out):
-    c, i = pl.program_id(0), pl.program_id(1)
-
-    @pl.loop(0, 4 * LT)
-    def _(n):
-        l, b = n // 4, lax.rem(n, 4)
-        cols = pl.ds(pl.multiple_of(l * 128, 128), 128)
-        wide = pl.ds(pl.multiple_of(c * L + l * 128, 128), 128)
-        d = d_ref[0, pl.ds(pl.multiple_of(b * 128, 128), 144), cols].astype(F32)
-        result = sf_ref[i, 0:1, wide] * d[0:128]
-        for j in range(1, SHORT):
-            result = result + sf_ref[i, j : j + 1, wide] * d[j : j + 128]
-        gi_out[0, pl.ds(pl.multiple_of(b * 128, 128), 128), cols] = result.astype(BF16)
+ROWS = 256
+
+
+def finish_kernel(sf_ref, d_ref, more_ref, gl_ref, gs_ref, gi_out, gl_out, skip_out, gs_out, line):
+    i, b = pl.program_id(0), pl.program_id(1)
+
+    @pl.loop(0, CH // 512)
+    def _(quarter):
+        for k in range(4):
+            cols = pl.ds(pl.multiple_of(quarter * 512 + k * 128, 128), 128)
+            line[k, 0:ROWS] = d_ref[0, :, cols].astype(F32)
+            line[k, ROWS:] = more_ref[0, :, cols].astype(F32)
+        for k in range(4):
+            cols = pl.ds(pl.multiple_of(quarter * 512 + k * 128, 128), 128)
+            taps = [sf_ref[i, j : j + 1, cols] for j in range(SHORT)]
+
+            @pl.loop(0, ROWS // 64, unroll=4)
+            def _(r):
+                result = taps[0] * line[k, pl.ds(r * 64, 64)]
+                for j in range(1, SHORT):
+                    result = result + taps[j] * line[k, pl.ds(r * 64 + j, 64)]
+                gi_out[0, pl.ds(pl.multiple_of(r * 64, 64), 64), cols] = result.astype(BF16)
 
     @pl.when(i == 0)
     def _():
         gl_out[...] = gl_ref[...]
 
-    @pl.when(jnp.logical_and(c == 0, i == 0))
+    @pl.when(jnp.logical_and(i == 0, b == 0))
     def _():
-        skip_out[...] = top_ref[0]
+        skip_out[...] = gl_ref[0]
         for stream in range(3):
             for j in range(SHORT):
                 row = 3 * stream + j
@@ -481,10 +534,12 @@
 
 
 def finish(short_filters, d, gl, gs):
-    whole = lambda shape: pl.BlockSpec(shape, lambda c, i: (0,) * len(shape))
+    whole = lambda shape: pl.BlockSpec(shape, lambda i, b: (0,) * len(shape))
+    steps = TOK // ROWS
+    turn = pl.BlockSpec((TAPS // steps, CH), lambda i, b: (jnp.where(i == 0, b, steps - 1), 0))
     return pl.pallas_call(
         finish_kernel,
-        grid=(PARTS, 3),
+        grid=(3, steps),
         out_shape=(
             jax.ShapeDtypeStruct((3, TOK, CH), BF16),
             jax.ShapeDtypeStruct((TAPS, CH), F32),
@@ -493,20 +548,21 @@
         ),
         in_specs=[
             whole((3, SHORT, CH)),
-            pl.BlockSpec((1, TOK + 16, L), lambda c, i: (i, 0, c)),
-            pl.BlockSpec((TAPS, L), lambda c, i: (0, c)),
-            whole((8, CH)),
+            pl.BlockSpec((1, ROWS, CH), lambda i, b: (i, b, 0)),
+            pl.BlockSpec((1, 16, CH), lambda i, b: (i, (b + 1) * (ROWS // 16), 0)),
+            turn,
             whole((GROUP, 16, 128)),
         ],
         out_specs=(
-            pl.BlockSpec((1, TOK, L), lambda c, i: (i, 0, c)),
-            pl.BlockSpec((TAPS, L), lambda c, i: (0, c)),
+            pl.BlockSpec((1, ROWS, CH), lambda i, b: (i, b, 0)),
+            turn,
             whole((CH,)),
             whole((3, SHORT, CH)),
         ),
-        compiler_params=pltpu.CompilerParams(vmem_limit_bytes=24 << 20),
+        scratch_shapes=[pltpu.VMEM((4, ROWS + 16, 128), F32)],
+        compiler_params=pltpu.CompilerParams(vmem_limit_bytes=60 << 20),
         cost_estimate=pl.CostEstimate(flops=2 * 10**7, bytes_accessed=16 * 10**6, transcendentals=0),
-    )(short_filters, d, gl, gl, gs)
+    )(short_filters, d, d, gl, gs)
 
 
 def per_device(projected, short_filters, long_filter, skip_gain, cotangent):
@@ -535,6 +591,7 @@
         pltpu.VMEM((2 * POINTS, L), BF16),
         pltpu.VMEM((3 * TAPS, L), BF16),
         pltpu.VMEM((2 * TAPS, L), BF16),
+        pltpu.VMEM((3, TOK + 16, 128), F32),
         pltpu.VMEM((PARTS, TAPS, L), F32),
         *[pltpu.VMEM(m.shape, BF16) for m in mats],
         pltpu.VMEM((PARTS, TAPS, L), F32),

time: 101 us -> 92.5 us (0.916)
  the two profiles are of different devices: /device:TPU:6 before, /device:TPU:0 now
where the time goes in v4:
time: 92.5 us; the launch traced here: 92.2 us
  Pallas kernels  91.6 us (99%)
    pallas_call x1, Pallas kernels, per_device(): pl.pallas_call(kernel, out_shape=(jax.ShapeDtypeStruct((3, TOK + 16, CH),...  82.2 us
    pallas_call x1, Pallas kernels, finish(): pl.pallas_call(finish_kernel, grid=(3, steps), out_shape=(jax.ShapeDtypeS...  9.39 us

profile of v4, /device:TPU:0, one launch (start us, length us, event | category | flops | bytes accessed | tf_op | source)
XLA Modules:
  0.0 92.2 jit_solution(445819295018456984)
XLA Ops:
  0.6 82.2 %shard_map.156 = (bf16[3,528,2048]{2,1,0:T(8,128)(2,1)}, f32[128,2048]{1,0:T(8,128)}, f32[16,16,128]{2,1,0:T(8,128)}) custom-call(bf16[3,512,2048]{2,1,0:T(8,128)(2,1)} %proj.1, f32[3,3,2048]{2,1,0:T(4,128)} %sf_ref.3, f32[128,2048]{1,0:T(8,128)} %h_hbm.1, f32[1,2048]{1,0:T(1,128)} %bitcast.1, bf16[128,8192]{1,0:T(8,128)(2,1)} %cot_hbm.1, ...), custom_call_target="tpu_custom_call" | custom-call | flops 20000000000 | bytes 24000000 | tf_op jit(solution)/shard_map/pallas_call | solution.py:616
  82.9 9.4 %shard_map.157 = (bf16[3,512,2048]{2,1,0:T(8,128)(2,1)}, f32[128,2048]{1,0:T(8,128)}, f32[2048]{0:T(1024)}, f32[3,3,2048]{2,1,0:T(4,128)}) custom-call(f32[3,3,2048]{2,1,0:T(4,128)} %sf_ref.3, bf16[3,528,2048]{2,1,0:T(8,128)(2,1)} %get-tuple-element.7.d_ref.more_ref, bf16[3,528,2048]{2,1,0:T(8,128)(2,1)} %get-tuple-element.7.d_ref.more_ref, ...), custom_call_target="tpu_custom_call" | custom-call | flops 20000000 | bytes 16000000 | tf_op jit(solution)/shard_map/pallas_call | solution.py:540

commit v5 on v4

--- a/solution.py
+++ b/solution.py
@@ -62,7 +62,7 @@
     d_out, gl_out, gs_out,
     px, tip, p_halo_ref, qs, ks, vs, gated, g_halo, ghat, hhat, mixed, cot, dm, dm_halo, dhat, ds, d_halo,
     yb, hb, twice, line, hv, f0, f1, f2, f3, f4, f5, f6, f7,
-    parts, landed, xs, xr, sums, gs, gs_landed, gs_sums,
+    parts, landed, xs, xr, shared, sums, gs, gs_landed, gs_sums,
     load_sem, mat_sem, h_sem, own_sem, out_sem, halo_out_sem, a2a_send, a2a_recv,
     ph_sem, gh_sem, dmh_sem, dh_sem, rs_sem, xx_sem, ag_sem, tail_sem,
 ):
@@ -83,13 +83,6 @@
     def mate(k):
         return plane + lax.rem(g + k, GROUP)
 
-    @pl.loop(1, PEERS)
-    def _(k):
-        pl.semaphore_signal(barrier, inc=1, **to_seq(lax.rem(me + k, PEERS)))
-
-    for k in range(1, 4):
-        pl.semaphore_signal(barrier, inc=1, **to_ch(lax.rem(col + k, 4)))
-
     def lanes(c):
         return pl.ds(pl.multiple_of(c * L, L), L)
 
@@ -103,11 +96,16 @@
         pltpu.make_async_copy(a, b, mat_sem.at[i])
         for i, (a, b) in enumerate(zip((m0, m1, m2, m3, m4, m5, m6, m7), (f0, f1, f2, f3, f4, f5, f6, f7)))
     ]
-    for c in range(PARTS):
-        p_load(c).start()
-        h_load(c).start()
-    for m in mats:
-        m.start()
+    p_load(0).start()
+    p_load(1).start()
+
+    @pl.loop(1, PEERS)
+    def _(k):
+        pl.semaphore_signal(barrier, inc=1, **to_seq(lax.rem(me + k, PEERS)))
+
+    for k in range(1, 4):
+        pl.semaphore_signal(barrier, inc=1, **to_ch(lax.rem(col + k, 4)))
+
 
     def cot_block(c, owner):
         return cot.at[c, pl.ds(pl.multiple_of(owner * 128, 128), 128)]
@@ -148,7 +146,10 @@
             send_sem=dh_sem.at[0, c], recv_sem=dh_sem.at[1, c], **to_seq(prv))
 
     def d_store(c):
-        return pltpu.make_async_copy(ds.at[c, :, 0:TOK], d_out.at[:, 0:TOK, lanes(c)], out_sem.at[c])
+        return pltpu.make_async_copy(ds.at[c, 0:2, 0:TOK], d_out.at[0:2, 0:TOK, lanes(c)], out_sem.at[0, c])
+
+    def last_store(c):
+        return pltpu.make_async_copy(ds.at[c, 2, 0:TOK], d_out.at[2, 0:TOK, lanes(c)], out_sem.at[1, c])
 
     def halo_store(c):
         return pltpu.make_async_copy(d_halo.at[c], d_out.at[:, TOK : TOK + 16, lanes(c)], halo_out_sem.at[c])
@@ -185,6 +186,23 @@
     @pl.loop(0, PARTS)
     def _(c):
         p_load(c).wait()
+
+        @pl.when(c + 2 < PARTS)
+        def _():
+            p_load(c + 2).start()
+
+        @pl.when(c == 0)
+        def _():
+            h_load(0).start()
+            mats[4].start()
+
+        @pl.when(c == 1)
+        def _():
+            for i in (0, 1, 2, 5, 7, 6, 3):
+                mats[i].start()
+            for k in range(1, PARTS):
+                h_load(k).start()
+
         px[c, :, 0:16] = jnp.zeros((3, 16, L), BF16)
         last = [px[c, i, TOK : TOK + 16].astype(F32)[14:16] for i in range(3)]
         tip[c] = jnp.concatenate(last + [jnp.zeros((10, L), F32)], axis=0).astype(BF16)
@@ -206,8 +224,7 @@
         gated_halo(1).start()
 
     cot_start(1)
-    for m in mats:
-        m.wait()
+    mats[4].wait()
 
     def filter_transform(c):
         h_load(c).wait()
@@ -351,12 +368,13 @@
 
     def spread(c):
         cross(c).wait_recv()
-        sums[c, mine] = (xs[c] + xr[c]) * (1.0 / 128.0)
+        total = (xs[c] + xr[c]) * (1.0 / 128.0)
+        shared[c, g] = jnp.concatenate([total[:, : L // 2], total[:, L // 2 :]], axis=0).astype(BF16)
 
         @pl.loop(1, GROUP)
         def _(k):
             pltpu.make_async_remote_copy(
-                src_ref=sums.at[c, mine], dst_ref=sums.at[c, mine],
+                src_ref=shared.at[c, g], dst_ref=shared.at[c, g],
                 send_sem=ag_sem.at[0, c], recv_sem=ag_sem.at[1, c], **to_seq(mate(k))).start()
 
     def short_gradient(c):
@@ -399,7 +417,11 @@
                     send_sem=tail_sem.at[0], recv_sem=tail_sem.at[1], **to_seq(peer)).start()
 
     gs[...] = jnp.zeros(gs.shape, F32)
+    for i in (0, 1, 2, 5):
+        mats[i].wait()
     filter_and_mix(0)
+    for i in (7, 6, 3):
+        mats[i].wait()
 
     @pl.loop(0, PARTS + 2)
     def _(s):
@@ -447,6 +469,28 @@
         @pl.when(s >= 2)
         def _():
             short_gradient(s - 2)
+
+    @pl.loop(0, PARTS)
+    def _(c):
+        @pl.when(has_previous)
+        def _():
+            grad_halo(c).wait_send()
+
+        @pl.loop(0, LT)
+        def _(l):
+            cols = pl.ds(pl.multiple_of(l * 128, 128), 128)
+            wide = pl.ds(pl.multiple_of(c * L + l * 128, 128), 128)
+            line[0] = ds[c, 2, :, cols].astype(F32)
+            taps = [sf_ref[2, j : j + 1, wide] for j in range(SHORT)]
+
+            @pl.loop(0, TOK // 64, unroll=4)
+            def _(r):
+                result = taps[0] * line[0, pl.ds(r * 64, 64)]
+                for j in range(1, SHORT):
+                    result = result + taps[j] * line[0, pl.ds(r * 64 + j, 64)]
+                ds[c, 2, pl.ds(pl.multiple_of(r * 64, 64), 64), cols] = result.astype(BF16)
+
+        last_store(c).start()
 
     gs_landed[me] = gs[g]
     others = gs_landed.at[0 : PEERS - 1]
@@ -468,7 +512,12 @@
 
     @pl.loop(0, PARTS)
     def _(c):
-        pltpu.make_async_copy(landed.at[c], landed.at[c], ag_sem.at[1, c]).wait()
+        fifteen = shared.at[c, 0 : GROUP - 1]
+        pltpu.make_async_copy(fifteen, fifteen, ag_sem.at[1, c]).wait()
+        for p in range(GROUP):
+            piece = shared[c, p].astype(F32)
+            sums[c, 8 * p : 8 * p + 8, : L // 2] = piece[0:8]
+            sums[c, 8 * p : 8 * p + 8, L // 2 :] = piece[8:16]
         gl_store(c).start()
         for k in (2, 1, 3):
             cot_send(c, k).wait_send()
@@ -481,12 +530,12 @@
         @pl.when(has_previous)
         def _():
             mixed_halo(c).wait_send()
-            grad_halo(c).wait_send()
 
         cross(c).wait_send()
         pltpu.make_async_copy(landed.at[c], landed.at[c], rs_sem.at[0, c]).wait()
-        pltpu.make_async_copy(landed.at[c], landed.at[c], ag_sem.at[0, c]).wait()
+        pltpu.make_async_copy(fifteen, fifteen, ag_sem.at[0, c]).wait()
         d_store(c).wait()
+        last_store(c).wait()
         halo_store(c).wait()
         gl_store(c).wait()
 
@@ -502,22 +551,28 @@
 def finish_kernel(sf_ref, d_ref, more_ref, gl_ref, gs_ref, gi_out, gl_out, skip_out, gs_out, line):
     i, b = pl.program_id(0), pl.program_id(1)
 
-    @pl.loop(0, CH // 512)
-    def _(quarter):
-        for k in range(4):
-            cols = pl.ds(pl.multiple_of(quarter * 512 + k * 128, 128), 128)
-            line[k, 0:ROWS] = d_ref[0, :, cols].astype(F32)
-            line[k, ROWS:] = more_ref[0, :, cols].astype(F32)
-        for k in range(4):
-            cols = pl.ds(pl.multiple_of(quarter * 512 + k * 128, 128), 128)
-            taps = [sf_ref[i, j : j + 1, cols] for j in range(SHORT)]
-
-            @pl.loop(0, ROWS // 64, unroll=4)
-            def _(r):
-                result = taps[0] * line[k, pl.ds(r * 64, 64)]
-                for j in range(1, SHORT):
-                    result = result + taps[j] * line[k, pl.ds(r * 64 + j, 64)]
-                gi_out[0, pl.ds(pl.multiple_of(r * 64, 64), 64), cols] = result.astype(BF16)
+    @pl.when(i < 2)
+    def _():
+        @pl.loop(0, CH // 512)
+        def _(quarter):
+            for k in range(4):
+                cols = pl.ds(pl.multiple_of(quarter * 512 + k * 128, 128), 128)
+                line[k, 0:ROWS] = d_ref[0, :, cols].astype(F32)
+                line[k, ROWS:] = more_ref[0, :, cols].astype(F32)
+            for k in range(4):
+                cols = pl.ds(pl.multiple_of(quarter * 512 + k * 128, 128), 128)
+                taps = [sf_ref[i, j : j + 1, cols] for j in range(SHORT)]
+
+                @pl.loop(0, ROWS // 64, unroll=4)
+                def _(r):
+                    result = taps[0] * line[k, pl.ds(r * 64, 64)]
+                    for j in range(1, SHORT):
+                        result = result + taps[j] * line[k, pl.ds(r * 64 + j, 64)]
+                    gi_out[0, pl.ds(pl.multiple_of(r * 64, 64), 64), cols] = result.astype(BF16)
+
+    @pl.when(i == 2)
+    def _():
+        gi_out[...] = d_ref[...]
 
     @pl.when(i == 0)
     def _():
@@ -598,6 +653,7 @@
         pltpu.VMEM((PARTS, GROUP - 1, 8, L), F32),
         pltpu.VMEM((PARTS, 8, L), F32),
         pltpu.VMEM((PARTS, 8, L), F32),
+        pltpu.VMEM((PARTS, GROUP, 16, L // 2), BF16),
         pltpu.VMEM((PARTS, TAPS, L), F32),
         pltpu.VMEM((GROUP, 16, 128), F32),
         pltpu.VMEM((PEERS, 16, 128), F32),
@@ -606,7 +662,7 @@
         dma((len(mats),)),
         dma((PARTS,)),
         dma((PARTS,)),
-        dma((PARTS,)),
+        dma((2, PARTS)),
         dma((PARTS,)),
         dma((PARTS, 3)),
         dma((PARTS, 3)),

time: 92.5 us -> 86.1 us (0.931)
  Pallas kernels: 91.6 us -> 85.2 us
    pallas_call x1, Pallas kernels: 82.2 us -> 76.5 us  [per_device(): pl.pallas_call(kernel, out_shape=(jax.ShapeDtypeStruct((3, TOK + 16, CH),...]
where the time goes in v5:
time: 86.1 us; the launch traced here: 85.8 us
  Pallas kernels  85.2 us (99%)
    pallas_call x1, Pallas kernels, per_device(): pl.pallas_call(kernel, out_shape=(jax.ShapeDtypeStruct((3, TOK + 16, CH),...  76.5 us
    pallas_call x1, Pallas kernels, finish(): pl.pallas_call(finish_kernel, grid=(3, steps), out_shape=(jax.ShapeDtypeS...  8.73 us

profile of v5, /device:TPU:0, one launch (start us, length us, event | category | flops | bytes accessed | tf_op | source)
XLA Modules:
  0.0 85.8 jit_solution(12233437373616297020)
XLA Ops:
  0.6 76.5 %shard_map.156 = (bf16[3,528,2048]{2,1,0:T(8,128)(2,1)}, f32[128,2048]{1,0:T(8,128)}, f32[16,16,128]{2,1,0:T(8,128)}) custom-call(bf16[3,512,2048]{2,1,0:T(8,128)(2,1)} %proj.1, f32[3,3,2048]{2,1,0:T(4,128)} %sf_ref.3, f32[128,2048]{1,0:T(8,128)} %h_hbm.1, f32[1,2048]{1,0:T(1,128)} %bitcast.1, bf16[128,8192]{1,0:T(8,128)(2,1)} %cot_hbm.1, ...), custom_call_target="tpu_custom_call" | custom-call | flops 20000000000 | bytes 24000000 | tf_op jit(solution)/shard_map/pallas_call | solution.py:672
  77.1 8.7 %shard_map.157 = (bf16[3,512,2048]{2,1,0:T(8,128)(2,1)}, f32[128,2048]{1,0:T(8,128)}, f32[2048]{0:T(1024)}, f32[3,3,2048]{2,1,0:T(4,128)}) custom-call(f32[3,3,2048]{2,1,0:T(4,128)} %sf_ref.3, bf16[3,528,2048]{2,1,0:T(8,128)(2,1)} %get-tuple-element.7.d_ref.more_ref, bf16[3,528,2048]{2,1,0:T(8,128)(2,1)} %get-tuple-element.7.d_ref.more_ref, ...), custom_call_target="tpu_custom_call" | custom-call | flops 20000000 | bytes 16000000 | tf_op jit(solution)/shard_map/pallas_call | solution.py:595

commit v6 on v5

--- a/solution.py
+++ b/solution.py
@@ -145,11 +145,8 @@
             src_ref=ds.at[c, :, 0:16], dst_ref=d_halo.at[c],
             send_sem=dh_sem.at[0, c], recv_sem=dh_sem.at[1, c], **to_seq(prv))
 
-    def d_store(c):
-        return pltpu.make_async_copy(ds.at[c, 0:2, 0:TOK], d_out.at[0:2, 0:TOK, lanes(c)], out_sem.at[0, c])
-
-    def last_store(c):
-        return pltpu.make_async_copy(ds.at[c, 2, 0:TOK], d_out.at[2, 0:TOK, lanes(c)], out_sem.at[1, c])
+    def d_store(i, c):
+        return pltpu.make_async_copy(ds.at[c, i, 0:TOK], d_out.at[i, 0:TOK, lanes(c)], out_sem.at[i, c])
 
     def halo_store(c):
         return pltpu.make_async_copy(d_halo.at[c], d_out.at[:, TOK : TOK + 16, lanes(c)], halo_out_sem.at[c])
@@ -346,7 +343,7 @@
         grad = back(f6)
         ds[c, 1, 0:TOK] = (grad * vs[c]).astype(BF16)
         ds[c, 2, 0:TOK] = (grad * ks[c]).astype(BF16)
-        d_store(c).start()
+        d_store(0, c).start()
 
         @pl.when(has_previous)
         def _():
@@ -429,6 +426,10 @@
         def _():
             multiply_cotangent(s)
 
+        @pl.when(s < PARTS)
+        def _():
+            filter_gradient(s)
+
         @pl.when(s + 2 < PARTS)
         def _():
             @pl.when(has_next)
@@ -437,10 +438,6 @@
 
             cot_start(s + 2)
 
-        @pl.when(s < PARTS)
-        def _():
-            filter_gradient(s)
-
         @pl.when(s + 1 < PARTS)
         def _():
             filter_transform(s + 1)
@@ -470,28 +467,32 @@
         def _():
             short_gradient(s - 2)
 
-    @pl.loop(0, PARTS)
-    def _(c):
-        @pl.when(has_previous)
-        def _():
-            grad_halo(c).wait_send()
-
-        @pl.loop(0, LT)
-        def _(l):
+    def finish_stream(i):
+        @pl.loop(0, PARTS * LT)
+        def _(n):
+            c, l = n // LT, lax.rem(n, LT)
             cols = pl.ds(pl.multiple_of(l * 128, 128), 128)
-            wide = pl.ds(pl.multiple_of(c * L + l * 128, 128), 128)
-            line[0] = ds[c, 2, :, cols].astype(F32)
-            taps = [sf_ref[2, j : j + 1, wide] for j in range(SHORT)]
+            wide = pl.ds(pl.multiple_of(n * 128, 128), 128)
+            line[i] = ds[c, i, :, cols].astype(F32)
+            taps = [sf_ref[i, j : j + 1, wide] for j in range(SHORT)]
 
             @pl.loop(0, TOK // 64, unroll=4)
             def _(r):
-                result = taps[0] * line[0, pl.ds(r * 64, 64)]
+                result = taps[0] * line[i, pl.ds(r * 64, 64)]
                 for j in range(1, SHORT):
-                    result = result + taps[j] * line[0, pl.ds(r * 64 + j, 64)]
-                ds[c, 2, pl.ds(pl.multiple_of(r * 64, 64), 64), cols] = result.astype(BF16)
-
-        last_store(c).start()
-
+                    result = result + taps[j] * line[i, pl.ds(r * 64 + j, 64)]
+                ds[c, i, pl.ds(pl.multiple_of(r * 64, 64), 64), cols] = result.astype(BF16)
+
+            @pl.when(l == LT - 1)
+            def _():
+                d_store(i, c).start()
+
+    @pl.when(has_previous)
+    def _():
+        for c in range(PARTS):
+            grad_halo(c).wait_send()
+
+    finish_stream(2)
     gs_landed[me] = gs[g]
     others = gs_landed.at[0 : PEERS - 1]
     mates = gs_landed.at[0 : GROUP - 1]
@@ -506,6 +507,8 @@
         pltpu.make_async_remote_copy(
             src_ref=gs_sums.at[g], dst_ref=gs_sums.at[g],
             send_sem=tail_sem.at[2], recv_sem=tail_sem.at[3], **to_seq(mate(k))).start()
+
+    finish_stream(1)
 
     def gl_store(c):
         return pltpu.make_async_copy(sums.at[c], gl_out.at[:, lanes(c)], h_sem.at[c])
@@ -534,8 +537,8 @@
         cross(c).wait_send()
         pltpu.make_async_copy(landed.at[c], landed.at[c], rs_sem.at[0, c]).wait()
         pltpu.make_async_copy(fifteen, fifteen, ag_sem.at[0, c]).wait()
-        d_store(c).wait()
-        last_store(c).wait()
+        for i in range(3):
+            d_store(i, c).wait()
         halo_store(c).wait()
         gl_store(c).wait()
 
@@ -551,7 +554,7 @@
 def finish_kernel(sf_ref, d_ref, more_ref, gl_ref, gs_ref, gi_out, gl_out, skip_out, gs_out, line):
     i, b = pl.program_id(0), pl.program_id(1)
 
-    @pl.when(i < 2)
+    @pl.when(i < 1)
     def _():
         @pl.loop(0, CH // 512)
         def _(quarter):
@@ -570,7 +573,7 @@
                         result = result + taps[j] * line[k, pl.ds(r * 64 + j, 64)]
                     gi_out[0, pl.ds(pl.multiple_of(r * 64, 64), 64), cols] = result.astype(BF16)
 
-    @pl.when(i == 2)
+    @pl.when(i >= 1)
     def _():
         gi_out[...] = d_ref[...]
 
@@ -662,7 +665,7 @@
         dma((len(mats),)),
         dma((PARTS,)),
         dma((PARTS,)),
-        dma((2, PARTS)),
+        dma((3, PARTS)),
         dma((PARTS,)),
         dma((PARTS, 3)),
         dma((PARTS, 3)),

time: 86.1 us -> 85.1 us (0.988)
  Pallas kernels: 85.2 us -> 84.2 us
where the time goes in v6:
time: 85.1 us; the launch traced here: 84.8 us
  Pallas kernels  84.2 us (99%)
    pallas_call x1, Pallas kernels, per_device(): pl.pallas_call(kernel, out_shape=(jax.ShapeDtypeStruct((3, TOK + 16, CH),...  76.2 us
    pallas_call x1, Pallas kernels, finish(): pl.pallas_call(finish_kernel, grid=(3, steps), out_shape=(jax.ShapeDtypeS...  7.95 us

profile of v6, /device:TPU:0, one launch (start us, length us, event | category | flops | bytes accessed | tf_op | source)
XLA Modules:
  0.0 84.8 jit_solution(15628332928601902319)
XLA Ops:
  0.6 76.2 %shard_map.156 = (bf16[3,528,2048]{2,1,0:T(8,128)(2,1)}, f32[128,2048]{1,0:T(8,128)}, f32[16,16,128]{2,1,0:T(8,128)}) custom-call(bf16[3,512,2048]{2,1,0:T(8,128)(2,1)} %proj.1, f32[3,3,2048]{2,1,0:T(4,128)} %sf_ref.3, f32[128,2048]{1,0:T(8,128)} %h_hbm.1, f32[1,2048]{1,0:T(1,128)} %bitcast.1, bf16[128,8192]{1,0:T(8,128)(2,1)} %cot_hbm.1, ...), custom_call_target="tpu_custom_call" | custom-call | flops 20000000000 | bytes 24000000 | tf_op jit(solution)/shard_map/pallas_call | solution.py:675
  76.9 8.0 %shard_map.157 = (bf16[3,512,2048]{2,1,0:T(8,128)(2,1)}, f32[128,2048]{1,0:T(8,128)}, f32[2048]{0:T(1024)}, f32[3,3,2048]{2,1,0:T(4,128)}) custom-call(f32[3,3,2048]{2,1,0:T(4,128)} %sf_ref.3, bf16[3,528,2048]{2,1,0:T(8,128)(2,1)} %get-tuple-element.7.d_ref.more_ref, bf16[3,528,2048]{2,1,0:T(8,128)(2,1)} %get-tuple-element.7.d_ref.more_ref, ...), custom_call_target="tpu_custom_call" | custom-call | flops 20000000 | bytes 16000000 | tf_op jit(solution)/shard_map/pallas_call | solution.py:598

commit v7 on v6

--- a/solution.py
+++ b/solution.py
@@ -436,12 +436,14 @@
             def _():
                 gated_halo(s + 2).start()
 
-            cot_start(s + 2)
-
         @pl.when(s + 1 < PARTS)
         def _():
             filter_transform(s + 1)
             filter_and_mix(s + 1)
+
+        @pl.when(s + 2 < PARTS)
+        def _():
+            cot_start(s + 2)
 
         @pl.when(jnp.logical_and(s >= 2, s <= PARTS))
         def _():

time: 85.1 us -> 87.6 us (1.029)
  Pallas kernels: 84.2 us -> 86.7 us
    pallas_call x1, Pallas kernels: 76.2 us -> 78.7 us  [per_device(): pl.pallas_call(kernel, out_shape=(jax.ShapeDtypeStruct((3, TOK + 16, CH),...]
where the time goes in v7:
time: 87.6 us; the launch traced here: 87.3 us
  Pallas kernels  86.7 us (99%)
    pallas_call x1, Pallas kernels, per_device(): pl.pallas_call(kernel, out_shape=(jax.ShapeDtypeStruct((3, TOK + 16, CH),...  78.7 us
    pallas_call x1, Pallas kernels, finish(): pl.pallas_call(finish_kernel, grid=(3, steps), out_shape=(jax.ShapeDtypeS...  7.95 us

profile of v7, /device:TPU:0, one launch (start us, length us, event | category | flops | bytes accessed | tf_op | source)
XLA Modules:
  0.0 87.3 jit_solution(4165588467278366705)
XLA Ops:
  0.6 78.7 %shard_map.156 = (bf16[3,528,2048]{2,1,0:T(8,128)(2,1)}, f32[128,2048]{1,0:T(8,128)}, f32[16,16,128]{2,1,0:T(8,128)}) custom-call(bf16[3,512,2048]{2,1,0:T(8,128)(2,1)} %proj.1, f32[3,3,2048]{2,1,0:T(4,128)} %sf_ref.3, f32[128,2048]{1,0:T(8,128)} %h_hbm.1, f32[1,2048]{1,0:T(1,128)} %bitcast.1, bf16[128,8192]{1,0:T(8,128)(2,1)} %cot_hbm.1, ...), custom_call_target="tpu_custom_call" | custom-call | flops 20000000000 | bytes 24000000 | tf_op jit(solution)/shard_map/pallas_call | solution.py:677
  79.4 8.0 %shard_map.157 = (bf16[3,512,2048]{2,1,0:T(8,128)(2,1)}, f32[128,2048]{1,0:T(8,128)}, f32[2048]{0:T(1024)}, f32[3,3,2048]{2,1,0:T(4,128)}) custom-call(f32[3,3,2048]{2,1,0:T(4,128)} %sf_ref.3, bf16[3,528,2048]{2,1,0:T(8,128)(2,1)} %get-tuple-element.7.d_ref.more_ref, bf16[3,528,2048]{2,1,0:T(8,128)(2,1)} %get-tuple-element.7.d_ref.more_ref, ...), custom_call_target="tpu_custom_call" | custom-call | flops 20000000 | bytes 16000000 | tf_op jit(solution)/shard_map/pallas_call | solution.py:600
